TPU v7x, 512 devices: a whole 4x8x8 slice. The times are simulated.
512 devices in a mesh: pas: 64 (over z, y), qry: 8 (over x, core).
Axes of the slice: x: 4, y: 8, z: 8, core: 2. Of those that a mesh axis runs over, the one named last changes fastest.
Arguments:
- queries: bfloat16 [65536, 4096], P(('pas', 'qry')), as said below
- grad_out: bfloat16 [65536, 4096], P(('pas', 'qry')), may hold values from -6 to 6
- suffix_keys: bfloat16 [65536, 512], P(('pas', 'qry')), may hold values from -6 to 6
- suffix_values: bfloat16 [65536, 512], P(('pas', 'qry')), may hold values from -6 to 6
- passage_keys: bfloat16 [1024, 4, 512], P('pas'), as said below
- passage_values: bfloat16 [1024, 4, 512], P('pas'), may hold values from -6 to 6
- passage_lengths: int32 [1024], P('pas'), may hold values from 1 to 4
- retrieved: int32 [1024, 32], P(('pas', 'qry')), may hold values from 0 to 1023, as said below
Outputs:
- grad_queries: bfloat16 [65536, 4096], P(('pas', 'qry'))
- grad_suffix_keys: bfloat16 [65536, 512], P(('pas', 'qry'))
- grad_suffix_values: bfloat16 [65536, 512], P(('pas', 'qry'))
- grad_passage_keys: bfloat16 [1024, 4, 512], P(('pas', 'qry'))
- grad_passage_values: bfloat16 [1024, 4, 512], P(('pas', 'qry'))
Inputs may be any that keep to these rules, and one draw needn't show every extreme that they name: `queries`: entries stay within -6 to 6. `passage_keys`: entries stay within -6 to 6. `retrieved`: passage m belongs to owner m // 16. The 2 rows of one device (aligned blocks of 2 rows) hold only different ids, and at most 2 of them belong to one owner; in every block some owner has exactly 2.
All inputs are finite; a program needn't handle non-finite values.
Results may differ from a plain program's by a relative error of at most 0.0085.
Values may be sent and summed in bfloat16 or wider, within the bound.
No kernel may reach another device: no remote copies, remote signals or barrier semaphores. Data moves between devices by JAX's collectives and lax.ppermute only.
A program may use at most 64 MiB of HBM per device.

v0:
```python
import math

import jax
import jax.numpy as jnp
from jax import lax
from jax.sharding import PartitionSpec as P

HQ = 32
HD = 128


def score_weights(query_block, key_rows, allowed, score_scale):
    scores = (
        jnp.einsum("igxd,jgd->gxij", query_block, key_rows, preferred_element_type=jnp.float32)
        * score_scale
    )
    scores = jnp.where(allowed[None, None], scores, -jnp.inf)
    row_top = jnp.max(scores, axis=-1, keepdims=True)
    raised = jnp.exp(scores - row_top)
    return raised / jnp.sum(raised, axis=-1, keepdims=True)


def gradients(probabilities, query_block, grad_block, key_rows, value_rows, score_scale):
    weights = probabilities.astype(jnp.bfloat16)
    attended = jnp.einsum("gxij,jgd->igxd", weights, value_rows, preferred_element_type=jnp.float32)
    row_delta = jnp.sum(grad_block.astype(jnp.float32) * attended, axis=-1)
    prob_grad = jnp.einsum(
        "igxd,jgd->gxij", grad_block, value_rows, preferred_element_type=jnp.float32
    )
    dscore = (probabilities * (prob_grad - jnp.transpose(row_delta, (1, 2, 0))[..., None])).astype(
        jnp.bfloat16
    )
    grad_query = (
        jnp.einsum("gxij,jgd->igxd", dscore, key_rows, preferred_element_type=jnp.float32)
        * score_scale
    )
    grad_key = (
        jnp.einsum("gxij,igxd->jgd", dscore, query_block, preferred_element_type=jnp.float32)
        * score_scale
    )
    grad_value = jnp.einsum(
        "gxij,igxd->jgd", weights, grad_block, preferred_element_type=jnp.float32
    )
    return (grad_query, grad_key, grad_value)


def on_device(
    queries,
    grad_out,
    suffix_keys,
    suffix_values,
    passage_keys,
    passage_values,
    passage_lengths,
    retrieved,
):
    owners = lax.axis_size("pas")
    n_local, passage_len, kv_width = passage_keys.shape
    n_query, n_ret = retrieved.shape
    q_len = queries.shape[0] // n_query
    kv_heads = kv_width // HD
    group_size = HQ // kv_heads
    capacity = max(2, (n_query * n_ret + owners - 1) // owners)
    slot_count = owners * capacity
    passage_rows = n_ret * passage_len
    score_scale = 1.0 / math.sqrt(HD)
    flat_ids = retrieved.reshape(-1)
    owner_of = flat_ids // n_local
    local_of = flat_ids - owner_of * n_local
    request_order = jnp.arange(flat_ids.shape[0])
    earlier = (owner_of[:, None] == owner_of[None, :]) & (
        request_order[None, :] < request_order[:, None]
    )
    slot_of = owner_of * capacity + jnp.sum(earlier, axis=1)
    placed = slot_of[:, None] == jnp.arange(slot_count, dtype=jnp.int32)[None, :]
    wanted = jnp.sum(jnp.where(placed, local_of[:, None] + 1, 0), axis=0) - 1
    asked_ids = lax.all_to_all(
        wanted.reshape(owners, capacity), "pas", split_axis=0, concat_axis=0, tiled=True
    ).reshape(-1)
    picked = jnp.maximum(asked_ids, 0)
    every_length = lax.all_gather(passage_lengths, "pas", axis=0, tiled=True)
    passage_total = every_length.shape[0]
    lookup = flat_ids[:, None] == jnp.arange(passage_total, dtype=jnp.int32)[None, :]
    lengths_of = jnp.sum(jnp.where(lookup, every_length[None, :], 0), axis=1)
    key_send = passage_keys[picked].reshape(owners, capacity, passage_len, kv_width)
    value_send = passage_values[picked].reshape(owners, capacity, passage_len, kv_width)
    key_slots, value_slots = (
        lax.all_to_all(key_send, "pas", split_axis=0, concat_axis=0, tiled=True),
        lax.all_to_all(value_send, "pas", split_axis=0, concat_axis=0, tiled=True),
    )
    key_slots = key_slots.reshape(slot_count, passage_len, kv_width)
    positions = jnp.arange(passage_len, dtype=jnp.int32)
    suffix_positions = jnp.arange(q_len, dtype=jnp.int32)
    causal = suffix_positions[None, :] <= suffix_positions[:, None]
    query_blocks = []
    key_lists = []
    prob_list = []
    for query_index in range(n_query):
        row_first = query_index * q_len
        slot_use = slot_of[query_index * n_ret : (query_index + 1) * n_ret]
        query_block = queries[row_first : row_first + q_len].reshape(
            q_len, kv_heads, group_size, HD
        )
        own_keys = suffix_keys[row_first : row_first + q_len].reshape(q_len, kv_heads, HD)
        key_rows = jnp.concatenate(
            [key_slots[slot_use].reshape(passage_rows, kv_heads, HD), own_keys], axis=0
        )
        live_keys = (
            positions[None, :] < lengths_of[query_index * n_ret : (query_index + 1) * n_ret, None]
        ).reshape(-1)
        allowed = jnp.concatenate(
            [jnp.broadcast_to(live_keys[None, :], (q_len, passage_rows)), causal], axis=1
        )
        query_blocks.append(query_block)
        key_lists.append(key_rows)
        prob_list.append(score_weights(query_block, key_rows, allowed, score_scale))
    value_slots = value_slots.reshape(slot_count, passage_len, kv_width)
    key_grad_slots = jnp.zeros((slot_count, passage_len, kv_width), jnp.bfloat16)
    value_grad_slots = jnp.zeros((slot_count, passage_len, kv_width), jnp.bfloat16)
    grad_rows = []
    suffix_key_rows = []
    suffix_value_rows = []
    for query_index in range(n_query):
        row_first = query_index * q_len
        slot_use = slot_of[query_index * n_ret : (query_index + 1) * n_ret]
        grad_block = grad_out[row_first : row_first + q_len].reshape(
            q_len, kv_heads, group_size, HD
        )
        own_values = suffix_values[row_first : row_first + q_len].reshape(q_len, kv_heads, HD)
        value_rows = jnp.concatenate(
            [value_slots[slot_use].reshape(passage_rows, kv_heads, HD), own_values], axis=0
        )
        grad_query, grad_key, grad_value = gradients(
            prob_list[query_index],
            query_blocks[query_index],
            grad_block,
            key_lists[query_index],
            value_rows,
            score_scale,
        )
        key_grad_slots = key_grad_slots.at[slot_use].set(
            grad_key[:passage_rows].reshape(n_ret, passage_len, kv_width).astype(jnp.bfloat16)
        )
        value_grad_slots = value_grad_slots.at[slot_use].set(
            grad_value[:passage_rows].reshape(n_ret, passage_len, kv_width).astype(jnp.bfloat16)
        )
        grad_rows.append(grad_query.reshape(q_len, HQ * HD).astype(jnp.bfloat16))
        suffix_key_rows.append(
            grad_key[passage_rows:].reshape(q_len, kv_width).astype(jnp.bfloat16)
        )
        suffix_value_rows.append(
            grad_value[passage_rows:].reshape(q_len, kv_width).astype(jnp.bfloat16)
        )
    back_keys, back_values = (
        lax.all_to_all(
            key_grad_slots.reshape(owners, capacity, passage_len, kv_width),
            "pas",
            split_axis=0,
            concat_axis=0,
            tiled=True,
        ),
        lax.all_to_all(
            value_grad_slots.reshape(owners, capacity, passage_len, kv_width),
            "pas",
            split_axis=0,
            concat_axis=0,
            tiled=True,
        ),
    )
    owner_table = (asked_ids[None, :] == jnp.arange(n_local, dtype=jnp.int32)[:, None]).astype(
        jnp.float32
    )
    flat_keys = back_keys.reshape(slot_count, passage_len * kv_width).astype(jnp.float32)
    flat_values = back_values.reshape(slot_count, passage_len * kv_width).astype(jnp.float32)
    total_keys = jnp.dot(
        owner_table, flat_keys, precision=lax.Precision.HIGHEST, preferred_element_type=jnp.float32
    ).reshape(n_local, passage_len, kv_width)
    total_values = jnp.dot(
        owner_table,
        flat_values,
        precision=lax.Precision.HIGHEST,
        preferred_element_type=jnp.float32,
    ).reshape(n_local, passage_len, kv_width)
    share_keys, share_values = (
        lax.psum_scatter(total_keys, "qry", scatter_dimension=0, tiled=True),
        lax.psum_scatter(total_values, "qry", scatter_dimension=0, tiled=True),
    )
    return (
        jnp.concatenate(grad_rows, axis=0),
        jnp.concatenate(suffix_key_rows, axis=0),
        jnp.concatenate(suffix_value_rows, axis=0),
        share_keys.astype(jnp.bfloat16),
        share_values.astype(jnp.bfloat16),
    )


def solution(mesh):
    in_specs = (
        P(("pas", "qry"), None),
        P(("pas", "qry"), None),
        P(("pas", "qry"), None),
        P(("pas", "qry"), None),
        P("pas", None, None),
        P("pas", None, None),
        P("pas"),
        P(("pas", "qry"), None),
    )
    out_specs = (
        P(("pas", "qry"), None),
        P(("pas", "qry"), None),
        P(("pas", "qry"), None),
        P(("pas", "qry"), None, None),
        P(("pas", "qry"), None, None),
    )
    return jax.shard_map(
        on_device, mesh=mesh, in_specs=in_specs, out_specs=out_specs, check_vma=False
    )
```

profile of v0, /device:TPU:1, one launch (start us, length us, event | category | flops | bytes accessed | tf_op | source)
XLA Modules:
  0.0 193.6 jit_solution(8044342608669958860)
XLA Ops:
  0.7 0.9 reshape.254
  1.8 0.8 sub.54
  2.6 17.1 %all-to-all-start = ((s32[64,1,2]{2,1,0:T(1,128)}), s32[64,1,2]{2,1,0:T(1,128)S(1)}, u32[]{:S(2)}, u32[]{:S(2)}) async-start(s32[64,1,2]{2,1,0:T(1,128)} %bitcast), calls=%async_computation | async-start | bytes 65536 | tf_op jit(solution)/shard_map/all_to_all | solution.py:77
  19.7 1.3 dynamic-slice
  21.7 0.9 dynamic-update-slice
  22.5 20.2 %all-reduce = s32[1024]{0:T(1024)S(1)} all-reduce(s32[1024]{0:T(1024)S(1)} %dynamic-update-slice), channel_id=1, replica_groups=mesh['pas'=64,'qry'=8] {'pas'}, use_global_device_ids=true, to_apply=%add | all-reduce | flops 1024 | bytes 8192
  43.4 0.5 broadcast.244
  43.9 0.8 fusion.80
  44.9 1.8 gather_fusion.2
  46.7 6.8 %all-to-all-start.2 = ((bf16[64,2,4,512]{3,2,1,0:T(4,128)(2,1)}), bf16[64,2,4,512]{3,2,1,0:T(4,128)(2,1)S(1)}, u32[]{:S(2)}, u32[]{:S(2)}) async-start(bf16[64,2,4,512]{3,2,1,0:T(4,128)(2,1)} %bitcast.8), calls=%async_computation.2 | async-start | bytes 1048576 | tf_op jit(solution)/shard_map/all_to_all | solution.py:89
  53.6 0.9 copy.129
  54.5 0.9 copy.132
  55.6 1.0 copy.133
  56.6 1.3 dynamic-slice.1
  58.6 0.6 pad_add_fusion.1
  59.3 1.8 gather_fusion
  61.1 7.1 %all-to-all-done.2 = bf16[64,2,4,512]{3,2,1,0:T(4,128)(2,1)S(1)} async-done(((bf16[64,2,4,512]{3,2,1,0:T(4,128)(2,1)}), bf16[64,2,4,512]{3,2,1,0:T(4,128)(2,1)S(1)}, u32[]{:S(2)}, u32[]{:S(2)}) %all-to-all-start.2) | async-done | bytes 524320 | tf_op jit(solution)/shard_map/all_to_all | solution.py:89
  68.2 5.2 %all-to-all-start.1 = ((bf16[64,2,4,512]{3,2,1,0:T(4,128)(2,1)}), bf16[64,2,4,512]{3,2,1,0:T(4,128)(2,1)S(1)}, u32[]{:S(2)}, u32[]{:S(2)}) async-start(bf16[64,2,4,512]{3,2,1,0:T(4,128)(2,1)} %bitcast.1), calls=%async_computation.1 | async-start | bytes 1048576 | tf_op jit(solution)/shard_map/all_to_all | solution.py:88
  73.5 0.7 copy_bitcast_fusion.7
  74.2 0.7 copy_bitcast_fusion.6
  74.8 0.7 eq.63
  75.5 0.7 gather_fusion.5
  76.2 0.7 gather_fusion.3
  76.9 10.8 %all-to-all-done.1 = bf16[64,2,4,512]{3,2,1,0:T(4,128)(2,1)S(1)} async-done(((bf16[64,2,4,512]{3,2,1,0:T(4,128)(2,1)}), bf16[64,2,4,512]{3,2,1,0:T(4,128)(2,1)S(1)}, u32[]{:S(2)}, u32[]{:S(2)}) %all-to-all-start.1) | async-done | bytes 524320 | tf_op jit(solution)/shard_map/all_to_all | solution.py:88
  87.7 0.7 gather_fusion.4
  88.4 1.3 gather_fusion.1
  89.8 0.7 copy.92
  90.5 2.1 %fusion.82 = (f32[4,8,64]{2,1,0:T(8,128)S(1)}, f32[4,8,64,192]{3,2,1,0:T(8,128)S(1)}) fusion(pred[64,192]{1,0:T(8,128)(4,1)} %get-tuple-element.30, bf16[64,4,8,128]{3,2,1,0:T(8,128)(2,1)} %bitcast.240, bf16[64,4,128]{2,0,1:T(8,128)(2,1)} %get-tuple-element.41, bf16[128,4,128]{2,0,1:T(8,128)(2,1)S(1)} %copy.89), kind=kOutput, calls=%fused_computation.148 | convolution fusion | flops 102629568 | bytes 2314240 | tf_op jit(solution)/shard_map/sub | solution.py:19
  92.7 0.3 fusion.33
  93.0 0.7 copy-done.10
  93.7 1.2 fusion.22
  94.9 0.6 fusion.13
  95.5 0.8 fusion.3
  96.5 1.2 fusion.25
  97.7 0.4 fusion.14
  98.3 2.1 %fusion.85 = (f32[4,8,64]{2,1,0:T(8,128)S(1)}, f32[4,8,64,192]{3,2,1,0:T(8,128)S(1)}) fusion(pred[64,192]{1,0:T(8,128)(4,1)} %get-tuple-element.29, bf16[64,4,8,128]{3,2,1,0:T(8,128)(2,1)} %bitcast.238, bf16[64,4,128]{2,0,1:T(8,128)(2,1)S(1)} %get-tuple-element.42, bf16[128,4,128]{2,0,1:T(8,128)(2,1)S(1)} %copy.81), kind=kOutput, calls=%fused_computation.149 | convolution fusion | flops 102629568 | bytes 2314240 | tf_op jit(solution)/shard_map/sub | solution.py:19
  100.4 0.3 fusion.32
  100.7 1.0 copy-done.2
  101.7 0.6 fusion.12
  102.3 0.8 fusion.5
  103.3 1.2 fusion.24
  104.5 0.4 fusion.15
  105.0 0.3 copy.96
  106.0 0.3 copy.88
  106.7 0.9 broadcast.192.clone
  107.6 4.0 %scatter_fusion = bf16[128,4,512]{2,1,0:T(4,128)(2,1)} fusion(bf16[128,4,512]{2,1,0:T(4,128)(2,1)} %broadcast.192.clone, s32[32]{0:T(128)S(1)} %copy-done.25, bf16[32,4,512]{2,1,0:T(4,128)(2,1)S(1)} %reshape.327), kind=kCustom, calls=%fused_computation.6 | custom fusion | bytes 393344 | tf_op jit(solution)/shard_map/scatter | solution.py:141
  111.6 4.0 %scatter_fusion.1 = bf16[128,4,512]{2,1,0:T(4,128)(2,1)} fusion(bf16[128,4,512]{2,1,0:T(4,128)(2,1)} %scatter_fusion, s32[32]{0:T(128)S(1)} %copy-done.23, bf16[32,4,512]{2,1,0:T(4,128)(2,1)S(1)} %reshape.335), kind=kCustom, calls=%fused_computation.7 | custom fusion | bytes 393344 | tf_op jit(solution)/shard_map/scatter | solution.py:141
  115.7 5.0 %all-to-all-start.3 = ((bf16[64,2,4,512]{3,2,1,0:T(4,128)(2,1)}), bf16[64,2,4,512]{3,2,1,0:T(4,128)(2,1)S(1)}, u32[]{:S(2)}, u32[]{:S(2)}) async-start(bf16[64,2,4,512]{3,2,1,0:T(4,128)(2,1)} %bitcast.41), calls=%async_computation.3 | async-start | bytes 1048576 | tf_op jit(solution)/shard_map/all_to_all | solution.py:155
  120.7 0.5 fusion.23
  121.2 0.6 copy-done.16
  122.0 0.9 broadcast.192.clone.1
  123.0 4.0 %scatter_fusion.2 = bf16[128,4,512]{2,1,0:T(4,128)(2,1)} fusion(bf16[128,4,512]{2,1,0:T(4,128)(2,1)} %broadcast.192.clone.1, s32[32]{0:T(128)S(1)} %copy-done.25, bf16[32,4,512]{2,1,0:T(4,128)(2,1)S(1)} %reshape.343), kind=kCustom, calls=%fused_computation.8 | custom fusion | bytes 393344 | tf_op jit(solution)/shard_map/scatter | solution.py:144
  127.0 4.0 %scatter_fusion.3 = bf16[128,4,512]{2,1,0:T(4,128)(2,1)} fusion(bf16[128,4,512]{2,1,0:T(4,128)(2,1)} %scatter_fusion.2, s32[32]{0:T(128)S(1)} %copy-done.23, bf16[32,4,512]{2,1,0:T(4,128)(2,1)S(1)} %reshape.351), kind=kCustom, calls=%fused_computation.9 | custom fusion | bytes 393344 | tf_op jit(solution)/shard_map/scatter | solution.py:144
  131.0 0.8 copy_bitcast_fusion.4
  131.9 0.7 pad_maximum_fusion.1
  132.6 2.2 %all-to-all-done.3 = bf16[64,2,4,512]{3,2,1,0:T(4,128)(2,1)S(1)} async-done(((bf16[64,2,4,512]{3,2,1,0:T(4,128)(2,1)}), bf16[64,2,4,512]{3,2,1,0:T(4,128)(2,1)S(1)}, u32[]{:S(2)}, u32[]{:S(2)}) %all-to-all-start.3) | async-done | bytes 524320 | tf_op jit(solution)/shard_map/all_to_all | solution.py:155
  134.8 9.7 %all-to-all-start.4 = ((bf16[64,2,4,512]{3,2,1,0:T(4,128)(2,1)}), bf16[64,2,4,512]{3,2,1,0:T(4,128)(2,1)S(1)}, u32[]{:S(2)}, u32[]{:S(2)}) async-start(bf16[64,2,4,512]{3,2,1,0:T(4,128)(2,1)} %bitcast.44), calls=%async_computation.4 | async-start | bytes 1048576 | tf_op jit(solution)/shard_map/all_to_all | solution.py:162
  144.5 0.9 copy_bitcast_fusion.3
  145.4 0.7 pad_maximum_fusion.2
  146.0 1.0 pad_maximum_fusion
  147.8 11.0 %all-to-all-done.4 = bf16[64,2,4,512]{3,2,1,0:T(4,128)(2,1)S(1)} async-done(((bf16[64,2,4,512]{3,2,1,0:T(4,128)(2,1)}), bf16[64,2,4,512]{3,2,1,0:T(4,128)(2,1)S(1)}, u32[]{:S(2)}, u32[]{:S(2)}) %all-to-all-start.4) | async-done | bytes 524320 | tf_op jit(solution)/shard_map/all_to_all | solution.py:162
  159.6 32.8 %all-reduce.5 = (bf16[16,4,512]{2,1,0:T(4,128)(2,1)S(1)}, bf16[16,4,512]{2,1,0:T(4,128)(2,1)S(1)}) all-reduce(f32[16,4,512]{2,1,0:T(4,128)S(1)} %copy.108, f32[16,4,512]{2,1,0:T(4,128)S(1)} %copy.112), channel_id=2, replica_groups=mesh['pas'=64,'qry'=8] {'qry'}, use_global_device_ids=true, to_apply=%region_11.12.clone | all-reduce | flops 65536 | bytes 393216
  192.4 0.6 dynamic-slice_convert_fusion.1
  193.0 0.6 dynamic-slice_convert_fusion
  (108 shorter events, 4.8 us)
Async XLA Ops:
  0.6 44.2 %copy-start = (bf16[16,4,512]{2,1,0:T(4,128)(2,1)S(1)}, bf16[16,4,512]{2,1,0:T(4,128)(2,1)}, u32[]{:S(2)}) copy-start(bf16[16,4,512]{2,1,0:T(4,128)(2,1)} %param.13) | copy-start | bytes 196612
  0.6 52.9 %copy-start.4 = (bf16[128,4096]{1,0:T(8,128)(2,1)S(1)}, bf16[128,4096]{1,0:T(8,128)(2,1)}, u32[]{:S(2)}) copy-start(bf16[128,4096]{1,0:T(8,128)(2,1)} %param.8) | copy-start | bytes 3145732
  2.6 40.8 %all-to-all-start = ((s32[64,1,2]{2,1,0:T(1,128)}), s32[64,1,2]{2,1,0:T(1,128)S(1)}, u32[]{:S(2)}, u32[]{:S(2)}) async-start(s32[64,1,2]{2,1,0:T(1,128)} %bitcast), calls=%async_computation | async-start | bytes 65536 | tf_op jit(solution)/shard_map/all_to_all | solution.py:77
  46.7 21.5 %all-to-all-start.2 = ((bf16[64,2,4,512]{3,2,1,0:T(4,128)(2,1)}), bf16[64,2,4,512]{3,2,1,0:T(4,128)(2,1)S(1)}, u32[]{:S(2)}, u32[]{:S(2)}) async-start(bf16[64,2,4,512]{3,2,1,0:T(4,128)(2,1)} %bitcast.8), calls=%async_computation.2 | async-start | bytes 1048576 | tf_op jit(solution)/shard_map/all_to_all | solution.py:89
  53.5 1.9 copy-start.5
  55.4 3.9 %copy-start.1 = (bf16[16,4,512]{2,1,0:T(4,128)(2,1)S(1)}, bf16[16,4,512]{2,1,0:T(4,128)(2,1)}, u32[]{:S(2)}) copy-start(bf16[16,4,512]{2,1,0:T(4,128)(2,1)} %param.12) | copy-start | bytes 196612
  55.5 17.9 %copy-start.17 = (bf16[128,512]{1,0:T(8,128)(2,1)S(1)}, bf16[128,512]{1,0:T(8,128)(2,1)}, u32[]{:S(2)}) copy-start(bf16[128,512]{1,0:T(8,128)(2,1)} %param.10) | copy-start | bytes 393220
  55.5 18.0 %copy-start.18 = (bf16[128,512]{1,0:T(8,128)(2,1)S(1)}, bf16[128,512]{1,0:T(8,128)(2,1)}, u32[]{:S(2)}) copy-start(bf16[128,512]{1,0:T(8,128)(2,1)} %param.11) | copy-start | bytes 393220
  55.6 46.6 %copy-start.6 = (bf16[8,8,32,128]{3,2,1,0:T(8,128)(2,1)}, bf16[8,8,32,128]{3,2,1,0:T(8,128)(2,1)S(1)}, u32[]{:S(2)}) copy-start(bf16[8,8,32,128]{3,2,1,0:T(8,128)(2,1)S(1)} %copy.130) | copy-start | bytes 1572868
  58.6 14.8 %copy-start.22 = (s32[32]{0:T(128)}, s32[32]{0:T(128)S(1)}, u32[]{:S(2)}) copy-start(s32[32]{0:T(128)S(1)} %get-tuple-element.32) | copy-start | bytes 388
  58.6 14.8 %copy-start.24 = (s32[32]{0:T(128)}, s32[32]{0:T(128)S(1)}, u32[]{:S(2)}) copy-start(s32[32]{0:T(128)S(1)} %get-tuple-element.31) | copy-start | bytes 388
  68.2 19.5 %all-to-all-start.1 = ((bf16[64,2,4,512]{3,2,1,0:T(4,128)(2,1)}), bf16[64,2,4,512]{3,2,1,0:T(4,128)(2,1)S(1)}, u32[]{:S(2)}, u32[]{:S(2)}) async-start(bf16[64,2,4,512]{3,2,1,0:T(4,128)(2,1)} %bitcast.1), calls=%async_computation.1 | async-start | bytes 1048576 | tf_op jit(solution)/shard_map/all_to_all | solution.py:88
  92.6 1.0 copy-start.10
  92.6 2.2 %copy-start.19 = (bf16[128,4,128]{2,0,1:T(8,128)(2,1)S(1)}, bf16[128,4,128]{2,0,1:T(8,128)(2,1)}, u32[]{:S(2)}) copy-start(bf16[128,4,128]{2,0,1:T(8,128)(2,1)} %copy.92) | copy-start | bytes 393220
  92.7 2.2 %copy-start.21 = (bf16[64,4,128]{2,0,1:T(8,128)(2,1)S(1)}, bf16[64,4,128]{2,0,1:T(8,128)(2,1)}, u32[]{:S(2)}) copy-start(bf16[64,4,128]{2,0,1:T(8,128)(2,1)} %get-tuple-element.45) | copy-start | bytes 196612
  95.5 1.0 copy-start.9
  96.5 1.2 copy-start.14
  96.5 1.7 copy-start.11
  100.4 1.3 copy-start.20
  100.7 1.0 copy-start.2
  102.3 1.0 copy-start.8
  104.5 1.0 copy-start.15
  104.5 1.2 slice-start
  105.5 1.0 slice-start.1
  105.7 1.9 copy-start.25
  105.9 5.8 %copy-start.23 = (s32[32]{0:T(128)S(1)}, s32[32]{0:T(128)}, u32[]{:S(2)}) copy-start(s32[32]{0:T(128)} %copy-done.22) | copy-start | bytes 388
  106.3 14.4 %copy-start.3 = (bf16[4,8,64,192]{3,2,1,0:T(8,128)(2,1)S(1)}, bf16[4,8,64,192]{3,2,1,0:T(8,128)(2,1)}, u32[]{:S(2)}) copy-start(bf16[4,8,64,192]{3,2,1,0:T(8,128)(2,1)} %copy-done.2) | copy-start | bytes 2359300
  106.3 14.4 %copy-start.7 = (bf16[8,8,32,128]{3,2,1,0:T(8,128)(2,1)S(1)}, bf16[8,8,32,128]{3,2,1,0:T(8,128)(2,1)}, u32[]{:S(2)}) copy-start(bf16[8,8,32,128]{3,2,1,0:T(8,128)(2,1)} %copy-done.6) | copy-start | bytes 1572868
  115.7 19.1 %all-to-all-start.3 = ((bf16[64,2,4,512]{3,2,1,0:T(4,128)(2,1)}), bf16[64,2,4,512]{3,2,1,0:T(4,128)(2,1)S(1)}, u32[]{:S(2)}, u32[]{:S(2)}) async-start(bf16[64,2,4,512]{3,2,1,0:T(4,128)(2,1)} %bitcast.41), calls=%async_computation.3 | async-start | bytes 1048576 | tf_op jit(solution)/shard_map/all_to_all | solution.py:155
  120.7 11.9 %copy-start.12 = (bf16[192,4,128]{2,0,1:T(8,128)(2,1)S(1)}, bf16[192,4,128]{2,0,1:T(8,128)(2,1)}, u32[]{:S(2)}) copy-start(bf16[192,4,128]{2,0,1:T(8,128)(2,1)} %fusion.22) | copy-start | bytes 589828
  121.2 0.7 copy-start.16
  121.2 10.7 %copy-start.13 = (bf16[192,4,128]{2,0,1:T(8,128)(2,1)S(1)}, bf16[192,4,128]{2,0,1:T(8,128)(2,1)}, u32[]{:S(2)}) copy-start(bf16[192,4,128]{2,0,1:T(8,128)(2,1)} %fusion.24) | copy-start | bytes 589828
  134.8 24.1 %all-to-all-start.4 = ((bf16[64,2,4,512]{3,2,1,0:T(4,128)(2,1)}), bf16[64,2,4,512]{3,2,1,0:T(4,128)(2,1)S(1)}, u32[]{:S(2)}, u32[]{:S(2)}) async-start(bf16[64,2,4,512]{3,2,1,0:T(4,128)(2,1)} %bitcast.44), calls=%async_computation.4 | async-start | bytes 1048576 | tf_op jit(solution)/shard_map/all_to_all | solution.py:162
  146.0 1.4 copy-start.26
where the time goes:
time: 196 us; the launch traced here: 194 us
  blocking collectives  53 us (27%)
  local copies, waits for them, and re-layouts  45.4 us (23%)
  starting transfers between devices  43.9 us (22%)
  waiting for transfers between devices  31.2 us (16%)
  matrix products  12.3 us (6%)
  other arithmetic  5.18 us (3%)
  between operations  2.7 us (1%)
    unnamed x2, blocking collectives  53 us
    all_to_all x1, starting transfers between devices, on_device(): lax.all_to_all(wanted.reshape(owners, capacity), 'pas', split_axis=0, con...  17.1 us
    all_to_all x1, waiting for transfers between devices, on_device(): lax.all_to_all(value_grad_slots.reshape(owners, capacity, passage_len, kv...  11 us
    all_to_all x1, waiting for transfers between devices, on_device(): lax.all_to_all(key_send, 'pas', split_axis=0, concat_axis=0, tiled=True)  10.8 us
    unnamed x70, local copies, waits for them, and re-layouts  9.92 us
    all_to_all x1, starting transfers between devices, on_device(): lax.all_to_all(value_grad_slots.reshape(owners, capacity, passage_len, kv...  9.74 us
    scatter x2, local copies, waits for them, and re-layouts, on_device(): value_grad_slots.at[slot_use]  8.07 us
    scatter x2, local copies, waits for them, and re-layouts, on_device(): key_grad_slots.at[slot_use]  8.03 us
  transfers between devices with their start and end apart: 5, of which 4 were waited for; matrix products, arithmetic and copies ran while one was open for 14% of the time, Pallas kernels for 0%

commit v1 on v0

v1 whole, which is shorter than its diff:
```python
import functools
import math

import jax
import jax.numpy as jnp
from jax import lax
from jax.experimental import pallas as pl
from jax.experimental.pallas import tpu as pltpu
from jax.sharding import PartitionSpec as P

HQ = 32
HD = 128
CAP = 2
DEAD = 16.0
NEG = -1e30
BF = jnp.bfloat16
F32 = jnp.float32


def iota(shape, dim):
    return lax.broadcasted_iota(jnp.int32, shape, dim)


def dot(a, b, ca=1, cb=0):
    return lax.dot_general(a, b, (((ca,), (cb,)), ((), ())), preferred_element_type=F32)


def one(mask, dtype=BF):
    return jnp.where(mask, 1.0, 0.0).astype(dtype)


def slot_masks(ids, owners, n_local, plen):
    n_query, n_ret = ids.shape
    lanes = n_ret * plen
    own = lax.div(ids, n_local)
    loc = ids - own * n_local
    spread = one(iota((n_ret, lanes), 1) // plen == iota((n_ret, lanes), 0), F32)
    own = dot(own.astype(F32), spread).astype(jnp.int32)
    loc = dot(loc.astype(F32), spread)
    before = one(
        (iota((lanes, lanes), 0) % plen == 0)
        & (iota((lanes, lanes), 0) // plen < iota((lanes, lanes), 1) // plen)
    )
    heads = one(iota((lanes, lanes), 0) % plen == 0)
    masks = []
    locals_ = []
    used = None
    for n in range(n_query):
        hit = iota((owners, lanes), 0) == own[n : n + 1]
        hit_b = one(hit)
        rank = dot(hit_b, before)
        if used is not None:
            rank = rank + used
        total = dot(hit_b, heads)
        used = total if used is None else used + total
        masks.append([one(hit & (rank == float(c)), F32) for c in range(CAP)])
        locals_.append(loc[n : n + 1])
    return masks, locals_


def request_kernel(owners, n_local, plen, ids_ref, req_ref):
    masks, locs = slot_masks(ids_ref[...], owners, n_local, plen)
    lanes = locs[0].shape[1]
    first = iota((owners, lanes), 1) % plen == 0
    wanted = []
    for c in range(CAP):
        total = 0.0
        for mask, loc in zip(masks, locs):
            total = total + mask[c] * (loc + 1.0)
        wanted.append(jnp.sum(jnp.where(first, total, 0.0), axis=1, keepdims=True))
    width = CAP * n_local * plen
    lane = iota((owners, width), 1)
    slot = lane // (n_local * plen)
    local = (lane % (n_local * plen)) // plen
    picked = jnp.where(slot == 0, wanted[0], wanted[1])
    req_ref[...] = one(picked == (local + 1).astype(F32), F32)


def owner_kernel(owners, n_local, plen, req_ref, len_ref, pk_ref, pv_ref, send_ref, table_ref):
    rows = owners * CAP * plen
    width = CAP * n_local * plen
    chunk = CAP * plen
    who = one(iota((rows, owners), 0) // chunk == iota((rows, owners), 1))
    spread = dot(who, req_ref[...].astype(BF))
    row = iota((rows, width), 0)
    lane = iota((rows, width), 1)
    same = ((row % chunk) // plen == lane // (n_local * plen)) & (row % plen == lane % plen)
    lane_row = iota((1, width), 1)
    lane_m = (lane_row % (n_local * plen)) // plen
    live = jnp.zeros((1, width), jnp.int32)
    for m in range(n_local):
        live = jnp.where(lane_m == m, len_ref[m], live)
    live = lane_row % plen < live
    table = jnp.where(same & live, spread, 0.0).astype(BF)
    table_ref[...] = table
    alive = dot(table, jnp.ones((width, HD), BF))
    fill = (1.0 - alive) * DEAD
    keys = jnp.concatenate([pk_ref[...]] * CAP, axis=0)
    values = jnp.concatenate([pv_ref[...]] * CAP, axis=0)
    kv_width = keys.shape[1]
    sent_keys = dot(table, keys)
    fill = jnp.concatenate([fill] * (kv_width // HD), axis=1)
    send_ref[:, :kv_width] = (sent_keys + fill).astype(BF)
    send_ref[:, kv_width:] = dot(table, values).astype(BF)


def attend_kernel(
    owners,
    n_local,
    plen,
    ids_ref,
    recv_ref,
    q_ref,
    g_ref,
    sk_ref,
    sv_ref,
    dq_ref,
    dsk_ref,
    dsv_ref,
    terms_ref,
    place_ref,
    kv_ref,
    out_ref,
):
    n_query, n_ret = ids_ref.shape
    lanes = n_ret * plen
    rows = owners * CAP * plen
    chunk = CAP * plen
    kv_width = sk_ref.shape[1]
    kv_heads = kv_width // HD
    group = HQ // kv_heads
    q_len = q_ref.shape[0] // n_query
    scale = 1.0 / math.sqrt(HD)
    log2e = 1.4426950408889634

    masks, _ = slot_masks(ids_ref[...], owners, n_local, plen)
    row = iota((rows, CAP * owners), 0)
    lane = iota((rows, CAP * owners), 1)
    who = one((row // chunk == lane % owners) & ((row % chunk) // plen == lane // owners))
    same = iota((rows, lanes), 0) % plen == iota((rows, lanes), 1) % plen
    for n in range(n_query):
        asked = jnp.concatenate([m.astype(BF) for m in masks[n]], axis=0)
        place_ref[:, n * lanes : (n + 1) * lanes] = jnp.where(same, dot(who, asked), 0.0).astype(BF)
    kv_ref[...] = dot(place_ref[...], recv_ref[...], 0, 0).astype(BF)

    causal = iota((q_len, group * q_len), 0) <= iota((q_len, group * q_len), 1) % q_len
    for g in range(kv_heads):
        col = g * HD
        vcol = kv_width + g * HD
        for n in range(n_query):
            r0 = n * q_len
            k0 = n * lanes
            q = jnp.concatenate(
                [
                    q_ref[r0 : r0 + q_len, (g * group + x) * HD : (g * group + x + 1) * HD]
                    for x in range(group)
                ],
                axis=0,
            )
            go = jnp.concatenate(
                [
                    g_ref[r0 : r0 + q_len, (g * group + x) * HD : (g * group + x + 1) * HD]
                    for x in range(group)
                ],
                axis=0,
            )
            pk = kv_ref[k0 : k0 + lanes, col : col + HD]
            keys = jnp.concatenate([pk, sk_ref[r0 : r0 + q_len, col : col + HD]], axis=0)
            values = jnp.concatenate(
                [kv_ref[k0 : k0 + lanes, vcol : vcol + HD], sv_ref[r0 : r0 + q_len, col : col + HD]],
                axis=0,
            )
            s = dot(keys, q, 1, 1) * (scale * log2e)
            alive = pk.astype(F32) < 0.5 * DEAD
            alive = jnp.concatenate([alive] * (group * q_len // HD), axis=1)
            s = jnp.concatenate(
                [jnp.where(alive, s[:lanes], NEG), jnp.where(causal, s[lanes:], NEG)], axis=0
            )
            e = jnp.exp2(s - jnp.max(s, axis=0, keepdims=True))
            p = e * (1.0 / jnp.sum(e, axis=0, keepdims=True))
            w = p.astype(BF)
            dp = dot(values, go, 1, 1)
            delta = jnp.sum(w.astype(F32) * dp, axis=0, keepdims=True)
            ds = (p * (dp - delta)).astype(BF)
            dv = dot(w, go)
            dk = dot(ds, q) * scale
            dq = (dot(ds, keys, 0, 0) * scale).astype(BF)
            for x in range(group):
                dq_ref[r0 : r0 + q_len, (g * group + x) * HD : (g * group + x + 1) * HD] = dq[
                    x * q_len : (x + 1) * q_len
                ]
            dsk_ref[r0 : r0 + q_len, col : col + HD] = dk[lanes:].astype(BF)
            dsv_ref[r0 : r0 + q_len, col : col + HD] = dv[lanes:].astype(BF)
            out_ref[k0 : k0 + lanes, col : col + HD] = dk[:lanes].astype(BF)
            out_ref[k0 : k0 + lanes, vcol : vcol + HD] = dv[:lanes].astype(BF)
    terms_ref[...] = dot(place_ref[...], out_ref[...]).astype(BF)


def owner_sum_kernel(table_ref, back_ref, sum_ref):
    total = dot(table_ref[...], back_ref[...], 0, 0)
    half = total.shape[0] // CAP
    sum_ref[...] = (total[:half] + total[half:]).astype(BF)


def final_kernel(parts_ref, gk_ref, gv_ref):
    total = jnp.sum(parts_ref[...].astype(F32), axis=0).astype(BF)
    n_out, plen, kv_width = gk_ref.shape
    for m in range(n_out):
        gk_ref[m] = total[m * plen : (m + 1) * plen, :kv_width]
        gv_ref[m] = total[m * plen : (m + 1) * plen, kv_width:]


VMEM = pl.BlockSpec(memory_space=pltpu.VMEM)
SMEM = pl.BlockSpec(memory_space=pltpu.SMEM)


def call(kernel, out_shape, in_specs, n_out, name, limit=16, scratch=()):
    return pl.pallas_call(
        kernel,
        out_shape=out_shape,
        in_specs=in_specs,
        out_specs=[VMEM] * n_out if n_out > 1 else VMEM,
        scratch_shapes=list(scratch),
        compiler_params=pltpu.CompilerParams(vmem_limit_bytes=limit * 2**20),
        name=name,
    )


def on_device(
    queries,
    grad_out,
    suffix_keys,
    suffix_values,
    passage_keys,
    passage_values,
    passage_lengths,
    retrieved,
):
    owners = lax.axis_size("pas")
    groups = lax.axis_size("qry")
    n_local, plen, kv_width = passage_keys.shape
    n_query, n_ret = retrieved.shape
    lanes = n_ret * plen
    rows = owners * CAP * plen
    width = CAP * n_local * plen
    sds = jax.ShapeDtypeStruct
    dims = (owners, n_local, plen)

    request = call(
        functools.partial(request_kernel, *dims), sds((owners, width), F32), [VMEM], 1, "request"
    )(retrieved)
    asked = lax.all_to_all(
        request.reshape(owners, 1, width), "pas", split_axis=0, concat_axis=0, tiled=True
    ).reshape(owners, width)

    flat_keys = passage_keys.reshape(n_local * plen, kv_width)
    flat_values = passage_values.reshape(n_local * plen, kv_width)
    send, table = call(
        functools.partial(owner_kernel, *dims),
        [sds((rows, 2 * kv_width), BF), sds((rows, width), BF)],
        [VMEM, SMEM, VMEM, VMEM],
        2,
        "owner_gather",
    )(asked, passage_lengths, flat_keys, flat_values)
    recv = lax.all_to_all(
        send.reshape(owners, CAP * plen, 2 * kv_width), "pas", split_axis=0, concat_axis=0, tiled=True
    ).reshape(rows, 2 * kv_width)

    dq, dsk, dsv, terms = call(
        functools.partial(attend_kernel, *dims),
        [
            sds(queries.shape, BF),
            sds(suffix_keys.shape, BF),
            sds(suffix_values.shape, BF),
            sds((rows, 2 * kv_width), BF),
        ],
        [VMEM] * 6,
        4,
        "attend",
        limit=32,
        scratch=[
            pltpu.VMEM((rows, n_query * lanes), BF),
            pltpu.VMEM((n_query * lanes, 2 * kv_width), BF),
            pltpu.VMEM((n_query * lanes, 2 * kv_width), BF),
        ],
    )(retrieved, recv, queries, grad_out, suffix_keys, suffix_values)
    back = lax.all_to_all(
        terms.reshape(owners, CAP * plen, 2 * kv_width), "pas", split_axis=0, concat_axis=0, tiled=True
    ).reshape(rows, 2 * kv_width)

    sums = call(owner_sum_kernel, sds((n_local * plen, 2 * kv_width), BF), [VMEM] * 2, 1, "owner_sum")(
        table, back
    )
    parts = lax.all_to_all(
        sums.reshape(groups, n_local // groups * plen, 2 * kv_width),
        "qry",
        split_axis=0,
        concat_axis=0,
        tiled=True,
    )
    out = sds((n_local // groups, plen, kv_width), BF)
    gk, gv = call(final_kernel, [out, out], [VMEM], 2, "final_sum")(parts)
    return dq, dsk, dsv, gk, gv


def solution(mesh):
    in_specs = (
        P(("pas", "qry"), None),
        P(("pas", "qry"), None),
        P(("pas", "qry"), None),
        P(("pas", "qry"), None),
        P("pas", None, None),
        P("pas", None, None),
        P("pas"),
        P(("pas", "qry"), None),
    )
    out_specs = (
        P(("pas", "qry"), None),
        P(("pas", "qry"), None),
        P(("pas", "qry"), None),
        P(("pas", "qry"), None, None),
        P(("pas", "qry"), None, None),
    )
    return jax.shard_map(
        on_device, mesh=mesh, in_specs=in_specs, out_specs=out_specs, check_vma=False
    )
```

time: 196 us -> 117 us (0.60)
  local copies, waits for them, and re-layouts: 45.4 us -> 2.21 us
  starting transfers between devices: 43.9 us -> 17.1 us
  blocking collectives: 53 us -> 77.9 us
  waiting for transfers between devices: 31.2 us -> 9.88 us
  matrix products: 12.3 us -> 0 us
  Pallas kernels: 0 us -> 8.51 us
  other arithmetic: 5.18 us -> 0 us
  between operations: 2.7 us -> 0.72 us
    all_to_all x0 -> x3, blocking collectives: none -> 77.9 us  [the longest x1 33.9 us: on_device(): lax.all_to_all(terms.reshape(owners, CAP * plen, 2 * kv_width), 'pas', sp...]
    unnamed x2 -> x0, blocking collectives: 53 us -> none
    all_to_all x5 -> x1, starting transfers between devices: 43.9 us -> 17.1 us  [on_device(): lax.all_to_all(request.reshape(owners, 1, width), 'pas', split_axis=0, co...]
    all_to_all x5 -> x1, waiting for transfers between devices: 31.2 us -> 9.88 us  [on_device(): lax.all_to_all(request.reshape(owners, 1, width), 'pas', split_axis=0, co...]
    scatter x4 -> x0, local copies, waits for them, and re-layouts: 16.1 us -> none  [the longest x2 8.07 us: on_device(): value_grad_slots.at[slot_use]]
    pallas_call x0 -> x5, Pallas kernels: none -> 8.51 us  [the longest x1 5.42 us: on_device(): call(functools.partial(attend_kernel, *dims), [sds(queries.shape, BF), sd...]
    dot_general x12 -> x0, matrix products: 8.11 us -> none  [the longest x2 2.36 us: gradients(): jnp.einsum('gxij,igxd->jgd', dscore, query_block, preferred_element_type=...]
    unnamed x70 -> x18, local copies, waits for them, and re-layouts: 9.92 us -> 2.17 us
  transfers between devices with their start and end apart: 5 -> 1, of which waited for: 4 -> 1; matrix products, arithmetic and copies ran while one was open for 14% -> 0% of each run, Pallas kernels for 0% -> 0%
where the time goes in v1:
time: 117 us; the launch traced here: 116 us
  blocking collectives  77.9 us (67%)
  starting transfers between devices  17.1 us (15%)
  waiting for transfers between devices  9.88 us (8%)
  Pallas kernels  8.51 us (7%)
  local copies, waits for them, and re-layouts  2.21 us (2%)
    all_to_all x1, blocking collectives, on_device(): lax.all_to_all(terms.reshape(owners, CAP * plen, 2 * kv_width), 'pas', sp...  33.9 us
    all_to_all x1, blocking collectives, on_device(): lax.all_to_all(send.reshape(owners, CAP * plen, 2 * kv_width), 'pas', spl...  29.7 us
    all_to_all x1, starting transfers between devices, on_device(): lax.all_to_all(request.reshape(owners, 1, width), 'pas', split_axis=0, co...  17.1 us
    all_to_all x1, blocking collectives, on_device(): lax.all_to_all(sums.reshape(groups, n_local // groups * plen, 2 * kv_widt...  14.3 us
    all_to_all x1, waiting for transfers between devices, on_device(): lax.all_to_all(request.reshape(owners, 1, width), 'pas', split_axis=0, co...  9.88 us
    pallas_call x1, Pallas kernels, on_device(): call(functools.partial(attend_kernel, *dims), [sds(queries.shape, BF), sd...  5.42 us
  transfers between devices with their start and end apart: 1, of which 1 were waited for; matrix products, arithmetic and copies ran while one was open for 0% of the time, Pallas kernels for 0%

profile of v1, /device:TPU:1, one launch (start us, length us, event | category | flops | bytes accessed | tf_op | source)
XLA Modules:
  0.0 116.4 jit_solution(6573949579224779418)
XLA Ops:
  0.6 0.0 copy-start.4
  0.6 0.7 copy-done.4
  1.3 0.0 copy-start.7
  1.3 1.0 request.1
  2.3 17.1 %all-to-all-start = ((f32[64,1,128]{2,1,0:T(1,128)}), f32[64,1,128]{2,1,0:T(1,128)S(1)}, u32[]{:S(2)}, u32[]{:S(2)}) async-start(f32[64,1,128]{2,1,0:T(1,128)} %bitcast.1), calls=%async_computation | async-start | bytes 65536 | tf_op jit(solution)/shard_map/all_to_all | solution.py:252
  19.4 0.0 copy-done.7
  19.5 0.0 copy-start.8
  19.5 0.8 copy-done.8
  20.3 0.0 copy-start.3
  20.3 0.0 copy-start.6
  20.3 9.9 %all-to-all-done = f32[64,1,128]{2,1,0:T(1,128)S(1)} async-done(((f32[64,1,128]{2,1,0:T(1,128)}), f32[64,1,128]{2,1,0:T(1,128)S(1)}, u32[]{:S(2)}, u32[]{:S(2)}) %all-to-all-start) | async-done | bytes 32800 | tf_op jit(solution)/shard_map/all_to_all | solution.py:252
  30.2 0.0 copy-done.6
  30.2 0.0 copy-start.2
  30.2 1.2 owner_gather.1
  31.4 0.0 copy-start
  31.4 0.0 copy-start.1
  31.4 29.7 %all_to_all.20 = bf16[64,8,1024]{2,1,0:T(8,128)(2,1)S(1)} all-to-all(bf16[64,8,1024]{2,1,0:T(8,128)(2,1)S(1)} %bitcast.11), channel_id=1, replica_groups=mesh['pas'=64,'qry'=8] {'pas'}, dimensions={0} | all-to-all | bytes 2097152 | tf_op jit(solution)/shard_map/all_to_all | solution.py:265
  61.1 0.0 copy-start.5
  61.1 0.0 copy-done.3
  61.1 0.0 copy-done.2
  61.1 0.0 copy-done
  61.1 0.0 copy-done.1
  61.1 0.7 copy-done.5
  61.7 5.4 %attend.1 = (bf16[128,4096]{1,0:T(8,128)(2,1)}, bf16[128,512]{1,0:T(8,128)(2,1)}, bf16[128,512]{1,0:T(8,128)(2,1)}, bf16[512,1024]{1,0:T(8,128)(2,1)S(1)}) custom-call(s32[2,32]{1,0:T(2,128)S(1)} %copy-done.5, bf16[512,1024]{1,0:T(8,128)(2,1)S(1)} %bitcast.10, bf16[128,4096]{1,0:T(8,128)(2,1)S(1)} %copy-done, bf16[128,4096]{1,0:T(8,128)(2,1)S(1)} %copy-done.1, ...), custom_call_target="tpu_custom_call" | custom-call | tf_op jit(solution)/shard_map/attend/pallas_call | solution.py:269
  67.2 33.9 %all_to_all.21 = bf16[64,8,1024]{2,1,0:T(8,128)(2,1)S(1)} all-to-all(bf16[64,8,1024]{2,1,0:T(8,128)(2,1)S(1)} %bitcast.12), channel_id=1, replica_groups=mesh['pas'=64,'qry'=8] {'pas'}, dimensions={0} | all-to-all | bytes 2097152 | tf_op jit(solution)/shard_map/all_to_all | solution.py:287
  101.1 0.3 owner_sum.1
  101.4 14.3 %all_to_all.22.parts_ref = bf16[8,8,1024]{2,1,0:T(8,128)(2,1)S(1)} all-to-all(bf16[8,8,1024]{2,1,0:T(8,128)(2,1)S(1)} %bitcast.13), channel_id=1, replica_groups=mesh['pas'=64,'qry'=8] {'qry'}, dimensions={0} | all-to-all | bytes 262144 | tf_op jit(solution)/shard_map/all_to_all | solution.py:294
  115.8 0.6 final_sum.1
  (2 shorter events, 0.0 us)
Async XLA Ops:
  0.6 0.7 copy-start.4
  1.3 18.1 %copy-start.7 = (bf16[16,4,512]{2,1,0:T(4,128)(2,1)S(1)}, bf16[16,4,512]{2,1,0:T(4,128)(2,1)}, u32[]{:S(2)}) copy-start(bf16[16,4,512]{2,1,0:T(4,128)(2,1)} %param.12) | copy-start | bytes 196612
  2.3 27.9 %all-to-all-start = ((f32[64,1,128]{2,1,0:T(1,128)}), f32[64,1,128]{2,1,0:T(1,128)S(1)}, u32[]{:S(2)}, u32[]{:S(2)}) async-start(f32[64,1,128]{2,1,0:T(1,128)} %bitcast.1), calls=%async_computation | async-start | bytes 65536 | tf_op jit(solution)/shard_map/all_to_all | solution.py:252
  19.5 0.8 copy-start.8
  20.3 40.8 %copy-start.3 = (bf16[128,512]{1,0:T(8,128)(2,1)S(1)}, bf16[128,512]{1,0:T(8,128)(2,1)}, u32[]{:S(2)}) copy-start(bf16[128,512]{1,0:T(8,128)(2,1)} %sv_ref.1) | copy-start | bytes 393220
  20.3 9.9 %copy-start.6 = (s32[16]{0:T(128)S(1)}, s32[16]{0:T(128)}, u32[]{:S(2)}) copy-start(s32[16]{0:T(128)} %len_ref.1) | copy-start | bytes 196
  30.2 30.8 %copy-start.2 = (bf16[128,512]{1,0:T(8,128)(2,1)S(1)}, bf16[128,512]{1,0:T(8,128)(2,1)}, u32[]{:S(2)}) copy-start(bf16[128,512]{1,0:T(8,128)(2,1)} %sk_ref.1) | copy-start | bytes 393220
  31.4 29.7 %copy-start = (bf16[128,4096]{1,0:T(8,128)(2,1)S(1)}, bf16[128,4096]{1,0:T(8,128)(2,1)}, u32[]{:S(2)}) copy-start(bf16[128,4096]{1,0:T(8,128)(2,1)} %q_ref.1) | copy-start | bytes 3145732
  31.4 29.7 %copy-start.1 = (bf16[128,4096]{1,0:T(8,128)(2,1)S(1)}, bf16[128,4096]{1,0:T(8,128)(2,1)}, u32[]{:S(2)}) copy-start(bf16[128,4096]{1,0:T(8,128)(2,1)} %g_ref.1) | copy-start | bytes 3145732
  61.1 0.7 copy-start.5

commit v2 on v1

v2 whole, which is shorter than its diff:
```python
import functools
import math

import jax
import jax.numpy as jnp
from jax import lax
from jax.experimental import pallas as pl
from jax.experimental.pallas import tpu as pltpu
from jax.sharding import PartitionSpec as P

HQ = 32
HD = 128
CAP = 2
DEAD = 16.0
NEG = -1e30
SCALE = 1.0 / math.sqrt(HD)
SCALE2 = SCALE * math.log2(math.e)
BF = jnp.bfloat16
F32 = jnp.float32


def iota(shape, dim):
    return lax.broadcasted_iota(jnp.int32, shape, dim)


def dot(a, b, ca=1, cb=0):
    return lax.dot_general(a, b, (((ca,), (cb,)), ((), ())), preferred_element_type=F32)


def one(mask, dtype=BF):
    return jnp.where(mask, 1.0, 0.0).astype(dtype)


def slot_masks(ids, owners, n_local, plen):
    n_query, n_ret = ids.shape
    lanes = n_ret * plen
    own = lax.div(ids, n_local)
    loc = ids - own * n_local
    spread = one(iota((n_ret, lanes), 1) // plen == iota((n_ret, lanes), 0), F32)
    own = dot(own.astype(F32), spread).astype(jnp.int32)
    loc = dot(loc.astype(F32), spread)
    before = one(
        (iota((lanes, lanes), 0) % plen == 0)
        & (iota((lanes, lanes), 0) // plen < iota((lanes, lanes), 1) // plen)
    )
    heads = one(iota((lanes, lanes), 0) % plen == 0)
    masks = []
    locals_ = []
    used = None
    for n in range(n_query):
        hit = iota((owners, lanes), 0) == own[n : n + 1]
        hit_b = one(hit)
        rank = dot(hit_b, before)
        if used is not None:
            rank = rank + used
        total = dot(hit_b, heads)
        used = total if used is None else used + total
        masks.append([one(hit & (rank == float(c)), F32) for c in range(CAP)])
        locals_.append(loc[n : n + 1])
    return masks, locals_


def request_kernel(owners, n_local, plen, ids_ref, req_ref):
    masks, locs = slot_masks(ids_ref[...], owners, n_local, plen)
    lanes = locs[0].shape[1]
    first = iota((owners, lanes), 1) % plen == 0
    wanted = []
    for c in range(CAP):
        total = 0.0
        for mask, loc in zip(masks, locs):
            total = total + mask[c] * (loc + 1.0)
        wanted.append(jnp.sum(jnp.where(first, total, 0.0), axis=1, keepdims=True))
    width = CAP * n_local * plen
    lane = iota((owners, width), 1)
    slot = lane // (n_local * plen)
    local = (lane % (n_local * plen)) // plen
    picked = jnp.where(slot == 0, wanted[0], wanted[1])
    req_ref[...] = one(picked == (local + 1).astype(F32), F32)


def owner_prepare_kernel(owners, n_local, plen, len_ref, pk_ref, pv_ref, mask_ref, kv_ref):
    rows = owners * CAP * plen
    width = CAP * n_local * plen
    chunk = CAP * plen
    row = iota((rows, width), 0)
    lane = iota((rows, width), 1)
    same = ((row % chunk) // plen == lane // (n_local * plen)) & (row % plen == lane % plen)
    lane_row = iota((1, width), 1)
    lane_m = (lane_row % (n_local * plen)) // plen
    live = jnp.zeros((1, width), jnp.int32)
    for m in range(n_local):
        live = jnp.where(lane_m == m, len_ref[m], live)
    live = lane_row % plen < live
    mask_ref[...] = one(same & live, F32)
    kv_width = pk_ref.shape[1]
    half = n_local * plen
    for c in range(CAP):
        kv_ref[c * half : (c + 1) * half, :kv_width] = pk_ref[...]
        kv_ref[c * half : (c + 1) * half, kv_width:] = pv_ref[...]


def owner_kernel(owners, plen, req_ref, mask_ref, kv_ref, send_ref, table_ref):
    rows, width = mask_ref.shape
    chunk = CAP * plen
    who = one(iota((rows, owners), 0) // chunk == iota((rows, owners), 1))
    spread = dot(who, req_ref[...].astype(BF))
    table = (spread * mask_ref[...]).astype(BF)
    table_ref[...] = table
    alive = dot(table, jnp.ones((width, HD), BF))
    fill = (1.0 - alive) * DEAD
    kv_width = kv_ref.shape[1] // 2
    sent = dot(table, kv_ref[...])
    for g in range(kv_width // HD):
        send_ref[:, g * HD : (g + 1) * HD] = (sent[:, g * HD : (g + 1) * HD] + fill).astype(BF)
    send_ref[:, kv_width:] = sent[:, kv_width:].astype(BF)


def attend_prepare_kernel(
    owners,
    n_local,
    plen,
    ids_ref,
    q_ref,
    g_ref,
    sk_ref,
    sv_ref,
    place_ref,
    qh_ref,
    gh_ref,
    s_ref,
    dp_ref,
):
    n_query, n_ret = ids_ref.shape
    lanes = n_ret * plen
    rows = owners * CAP * plen
    chunk = CAP * plen
    kv_heads = sk_ref.shape[1] // HD
    group = HQ // kv_heads
    q_len = q_ref.shape[0] // n_query

    masks, _ = slot_masks(ids_ref[...], owners, n_local, plen)
    row = iota((rows, CAP * owners), 0)
    lane = iota((rows, CAP * owners), 1)
    who = one((row // chunk == lane % owners) & ((row % chunk) // plen == lane // owners))
    same = iota((rows, lanes), 0) % plen == iota((rows, lanes), 1) % plen
    for n in range(n_query):
        asked = jnp.concatenate([m.astype(BF) for m in masks[n]], axis=0)
        place_ref[:, n * lanes : (n + 1) * lanes] = jnp.where(same, dot(who, asked), 0.0).astype(BF)

    causal = iota((q_len, group * q_len), 0) <= iota((q_len, group * q_len), 1) % q_len
    for n in range(n_query):
        r0 = n * q_len
        for g in range(kv_heads):
            at = n * kv_heads + g
            for x in range(group):
                col = (g * group + x) * HD
                qh_ref[at, x * q_len : (x + 1) * q_len] = q_ref[r0 : r0 + q_len, col : col + HD]
                gh_ref[at, x * q_len : (x + 1) * q_len] = g_ref[r0 : r0 + q_len, col : col + HD]
            keys = sk_ref[r0 : r0 + q_len, g * HD : (g + 1) * HD]
            values = sv_ref[r0 : r0 + q_len, g * HD : (g + 1) * HD]
            s = dot(keys, qh_ref[at], 1, 1) * SCALE2
            s_ref[at] = jnp.where(causal, s, NEG)
            dp_ref[at] = dot(values, gh_ref[at], 1, 1)


def attend_kernel(
    place_ref,
    recv_ref,
    qh_ref,
    gh_ref,
    s_ref,
    dp_ref,
    terms_ref,
    kv_ref,
    ds_ref,
    w_ref,
    out_ref,
):
    pairs, wide, _ = qh_ref.shape
    kv_width = recv_ref.shape[1] // 2
    kv_heads = kv_width // HD
    n_query = pairs // kv_heads
    lanes = place_ref.shape[1] // n_query
    kv_ref[...] = dot(place_ref[...], recv_ref[...], 0, 0).astype(BF)
    for n in range(n_query):
        k0 = n * lanes
        for g in range(kv_heads):
            at = n * kv_heads + g
            col = g * HD
            vcol = kv_width + g * HD
            q = qh_ref[at]
            go = gh_ref[at]
            pk = kv_ref[k0 : k0 + lanes, col : col + HD]
            pv = kv_ref[k0 : k0 + lanes, vcol : vcol + HD]
            alive = pk.astype(F32) < 0.5 * DEAD
            alive = jnp.concatenate([alive] * (wide // HD), axis=1)
            s_p = jnp.where(alive, dot(pk, q, 1, 1) * SCALE2, NEG)
            s_s = s_ref[at]
            top = jnp.maximum(
                jnp.max(s_p, axis=0, keepdims=True), jnp.max(s_s, axis=0, keepdims=True)
            )
            e_p = jnp.exp2(s_p - top)
            e_s = jnp.exp2(s_s - top)
            share = 1.0 / (
                jnp.sum(e_p, axis=0, keepdims=True) + jnp.sum(e_s, axis=0, keepdims=True)
            )
            p_p = e_p * share
            p_s = e_s * share
            w_p = p_p.astype(BF)
            w_s = p_s.astype(BF)
            dp_p = dot(pv, go, 1, 1)
            dp_s = dp_ref[at]
            delta = jnp.sum(w_p.astype(F32) * dp_p, axis=0, keepdims=True) + jnp.sum(
                w_s.astype(F32) * dp_s, axis=0, keepdims=True
            )
            ds_p = (p_p * (dp_p - delta)).astype(BF)
            ds_s = (p_s * (dp_s - delta)).astype(BF)
            out_ref[k0 : k0 + lanes, col : col + HD] = (dot(ds_p, q) * SCALE).astype(BF)
            out_ref[k0 : k0 + lanes, vcol : vcol + HD] = dot(w_p, go).astype(BF)
            ds_ref[at, :lanes] = ds_p
            ds_ref[at, lanes:] = ds_s
            w_ref[at] = w_s
    terms_ref[...] = dot(place_ref[...], out_ref[...]).astype(BF)


def attend_rest_kernel(kv_ref, ds_ref, w_ref, qh_ref, gh_ref, sk_ref, dq_ref, dsk_ref, dsv_ref):
    pairs, wide, _ = qh_ref.shape
    kv_heads = sk_ref.shape[1] // HD
    n_query = pairs // kv_heads
    lanes = kv_ref.shape[0] // n_query
    q_len = sk_ref.shape[0] // n_query
    group = wide // q_len
    for n in range(n_query):
        r0 = n * q_len
        for g in range(kv_heads):
            at = n * kv_heads + g
            col = g * HD
            ds = ds_ref[at]
            keys = jnp.concatenate(
                [
                    kv_ref[n * lanes : (n + 1) * lanes, col : col + HD],
                    sk_ref[r0 : r0 + q_len, col : col + HD],
                ],
                axis=0,
            )
            dq = (dot(ds, keys, 0, 0) * SCALE).astype(BF)
            for x in range(group):
                at_col = (g * group + x) * HD
                dq_ref[r0 : r0 + q_len, at_col : at_col + HD] = dq[x * q_len : (x + 1) * q_len]
            dsk = dot(ds[lanes:], qh_ref[at]) * SCALE
            dsk_ref[r0 : r0 + q_len, col : col + HD] = dsk.astype(BF)
            dsv_ref[r0 : r0 + q_len, col : col + HD] = dot(w_ref[at], gh_ref[at]).astype(BF)


def owner_sum_kernel(table_ref, back_ref, sum_ref):
    total = dot(table_ref[...], back_ref[...], 0, 0)
    half = total.shape[0] // CAP
    sum_ref[...] = (total[:half] + total[half:]).astype(BF)


def final_kernel(parts_ref, gk_ref, gv_ref):
    total = jnp.sum(parts_ref[...].astype(F32), axis=0).astype(BF)
    n_out, plen, kv_width = gk_ref.shape
    for m in range(n_out):
        gk_ref[m] = total[m * plen : (m + 1) * plen, :kv_width]
        gv_ref[m] = total[m * plen : (m + 1) * plen, kv_width:]


VMEM = pl.BlockSpec(memory_space=pltpu.VMEM)
SMEM = pl.BlockSpec(memory_space=pltpu.SMEM)


def call(kernel, out_shape, in_specs, name, limit=16, scratch=(), cost=None):
    several = isinstance(out_shape, (list, tuple))
    return pl.pallas_call(
        kernel,
        out_shape=out_shape,
        in_specs=in_specs,
        out_specs=[VMEM] * len(out_shape) if several else VMEM,
        scratch_shapes=list(scratch),
        compiler_params=pltpu.CompilerParams(vmem_limit_bytes=limit * 2**20),
        cost_estimate=cost,
        name=name,
    )


def cost(flops, mib, exps=0):
    return pl.CostEstimate(
        flops=int(flops), bytes_accessed=int(mib * 2**20), transcendentals=int(exps)
    )


def on_device(
    queries,
    grad_out,
    suffix_keys,
    suffix_values,
    passage_keys,
    passage_values,
    passage_lengths,
    retrieved,
):
    owners = lax.axis_size("pas")
    groups = lax.axis_size("qry")
    n_local, plen, kv_width = passage_keys.shape
    n_query, n_ret = retrieved.shape
    lanes = n_ret * plen
    rows = owners * CAP * plen
    width = CAP * n_local * plen
    kv_heads = kv_width // HD
    pairs = n_query * kv_heads
    q_len = queries.shape[0] // n_query
    wide = HQ // kv_heads * q_len
    sds = jax.ShapeDtypeStruct
    dims = (owners, n_local, plen)

    def exchange(x):
        parts = x.reshape((owners, rows // owners, x.shape[1]))
        return lax.all_to_all(parts, "pas", split_axis=0, concat_axis=0, tiled=True).reshape(x.shape)

    request = call(
        functools.partial(request_kernel, *dims), sds((owners, width), F32), [VMEM], "request"
    )(retrieved)
    asked = lax.all_to_all(
        request.reshape(owners, 1, width), "pas", split_axis=0, concat_axis=0, tiled=True
    ).reshape(owners, width)

    mask, tables = call(
        functools.partial(owner_prepare_kernel, *dims),
        [sds((rows, width), F32), sds((width, 2 * kv_width), BF)],
        [SMEM, VMEM, VMEM],
        "owner_prepare",
        cost=cost(1e6, 1),
    )(
        passage_lengths,
        passage_keys.reshape(n_local * plen, kv_width),
        passage_values.reshape(n_local * plen, kv_width),
    )
    send, table = call(
        functools.partial(owner_kernel, owners, plen),
        [sds((rows, 2 * kv_width), BF), sds((rows, width), BF)],
        [VMEM, VMEM, VMEM],
        "owner_gather",
    )(asked, mask, tables)
    recv = exchange(send)

    place, qh, gh, s_suf, dp_suf = call(
        functools.partial(attend_prepare_kernel, *dims),
        [
            sds((rows, n_query * lanes), BF),
            sds((pairs, wide, HD), BF),
            sds((pairs, wide, HD), BF),
            sds((pairs, q_len, wide), F32),
            sds((pairs, q_len, wide), F32),
        ],
        [VMEM] * 5,
        "attend_prepare",
        cost=cost(4 * pairs * wide * q_len * HD, 7),
    )(retrieved, queries, grad_out, suffix_keys, suffix_values)
    terms, kv, ds, w_suf = call(
        attend_kernel,
        [
            sds((rows, 2 * kv_width), BF),
            sds((n_query * lanes, 2 * kv_width), BF),
            sds((pairs, lanes + q_len, wide), BF),
            sds((pairs, q_len, wide), BF),
        ],
        [VMEM] * 6,
        "attend",
        scratch=[pltpu.VMEM((n_query * lanes, 2 * kv_width), BF)],
    )(place, recv, qh, gh, s_suf, dp_suf)
    back = exchange(terms)

    dq, dsk, dsv = call(
        attend_rest_kernel,
        [sds(queries.shape, BF), sds(suffix_keys.shape, BF), sds(suffix_values.shape, BF)],
        [VMEM] * 6,
        "attend_rest",
        cost=cost(8 * pairs * wide * (lanes + q_len) * HD, 6),
    )(kv, ds, w_suf, qh, gh, suffix_keys)

    sums = call(owner_sum_kernel, sds((n_local * plen, 2 * kv_width), BF), [VMEM] * 2, "owner_sum")(
        table, back
    )
    parts = lax.all_to_all(
        sums.reshape(groups, n_local // groups * plen, 2 * kv_width),
        "qry",
        split_axis=0,
        concat_axis=0,
        tiled=True,
    )
    out = sds((n_local // groups, plen, kv_width), BF)
    gk, gv = call(final_kernel, [out, out], [VMEM], "final_sum")(parts)
    return dq, dsk, dsv, gk, gv


def solution(mesh):
    in_specs = (
        P(("pas", "qry"), None),
        P(("pas", "qry"), None),
        P(("pas", "qry"), None),
        P(("pas", "qry"), None),
        P("pas", None, None),
        P("pas", None, None),
        P("pas"),
        P(("pas", "qry"), None),
    )
    out_specs = (
        P(("pas", "qry"), None),
        P(("pas", "qry"), None),
        P(("pas", "qry"), None),
        P(("pas", "qry"), None, None),
        P(("pas", "qry"), None, None),
    )
    return jax.shard_map(
        on_device, mesh=mesh, in_specs=in_specs, out_specs=out_specs, check_vma=False
    )
```

time: 117 us -> 121 us (1.034)
  blocking collectives: 77.9 us -> 34.1 us
  waiting for transfers between devices: 9.88 us -> 27.6 us
  starting transfers between devices: 17.1 us -> 31 us
  local copies, waits for them, and re-layouts: 2.21 us -> 14.7 us
  Pallas kernels: 8.51 us -> 12 us
    all_to_all x3 -> x1, blocking collectives: 77.9 us -> 34.1 us  [exchange(): lax.all_to_all(parts, 'pas', split_axis=0, concat_axis=0, tiled=True)]
    all_to_all x0 -> x2, waiting for transfers between devices: none -> 19.9 us  [the longest x1 19.1 us: exchange(): lax.all_to_all(parts, 'pas', split_axis=0, concat_axis=0, tiled=True)]
    all_to_all x0 -> x2, starting transfers between devices: none -> 13.9 us  [the longest x1 9.25 us: on_device(): lax.all_to_all(sums.reshape(groups, n_local // groups * plen, 2 * kv_widt...]
    unnamed x18 -> x38, local copies, waits for them, and re-layouts: 2.17 us -> 13 us
    pallas_call x3 -> x6, Pallas kernels: 7.2 us -> 10 us  [the longest x1 3.89 us: on_device(): call(attend_kernel, [sds((rows, 2 * kv_width), BF), sds((n_query * lanes,...]
    all_to_all x1, waiting for transfers between devices: 9.88 us -> 7.7 us  [on_device(): lax.all_to_all(request.reshape(owners, 1, width), 'pas', split_axis=0, co...]
    reshape x2, local copies, waits for them, and re-layouts: 0.04 us -> 1.72 us  [the longest x1 0.86 us: on_device(): passage_keys.reshape(n_local * plen, kv_width)]
  transfers between devices with their start and end apart: 1 -> 3, of which waited for: 1 -> 3; matrix products, arithmetic and copies ran while one was open for 0% -> 1% of each run, Pallas kernels for 0% -> 3%
where the time goes in v2:
time: 121 us; the launch traced here: 120 us
  blocking collectives  34.1 us (28%)
  starting transfers between devices  31 us (26%)
  waiting for transfers between devices  27.6 us (23%)
  local copies, waits for them, and re-layouts  14.7 us (12%)
  Pallas kernels  12 us (10%)
    all_to_all x1, blocking collectives, exchange(): lax.all_to_all(parts, 'pas', split_axis=0, concat_axis=0, tiled=True)  34.1 us
    all_to_all x1, waiting for transfers between devices, exchange(): lax.all_to_all(parts, 'pas', split_axis=0, concat_axis=0, tiled=True)  19.1 us
    all_to_all x1, starting transfers between devices, on_device(): lax.all_to_all(request.reshape(owners, 1, width), 'pas', split_axis=0, co...  17.1 us
    unnamed x38, local copies, waits for them, and re-layouts  13 us
    all_to_all x1, starting transfers between devices, on_device(): lax.all_to_all(sums.reshape(groups, n_local // groups * plen, 2 * kv_widt...  9.25 us
    all_to_all x1, waiting for transfers between devices, on_device(): lax.all_to_all(request.reshape(owners, 1, width), 'pas', split_axis=0, co...  7.7 us
    all_to_all x1, starting transfers between devices, exchange(): lax.all_to_all(parts, 'pas', split_axis=0, concat_axis=0, tiled=True)  4.65 us
    pallas_call x1, Pallas kernels, on_device(): call(attend_kernel, [sds((rows, 2 * kv_width), BF), sds((n_query * lanes,...  3.89 us
  transfers between devices with their start and end apart: 3, of which 3 were waited for; matrix products, arithmetic and copies ran while one was open for 1% of the time, Pallas kernels for 3%

profile of v2, /device:TPU:1, one launch (start us, length us, event | category | flops | bytes accessed | tf_op | source)
XLA Modules:
  0.0 120.2 jit_solution(5315600884687474664)
XLA Ops:
  0.6 0.0 copy-start.12
  0.6 0.0 copy-start.16
  0.7 0.7 copy-done.16
  1.4 0.0 copy-start.17
  1.4 1.0 request.1
  2.3 17.1 %all-to-all-start = ((f32[64,1,128]{2,1,0:T(1,128)}), f32[64,1,128]{2,1,0:T(1,128)S(1)}, u32[]{:S(2)}, u32[]{:S(2)}) async-start(f32[64,1,128]{2,1,0:T(1,128)} %bitcast.1), calls=%async_computation | async-start | bytes 65536 | tf_op jit(solution)/shard_map/all_to_all | solution.py:324
  19.5 0.9 reshape.39.pk_ref
  20.3 0.9 reshape.40.pv_ref
  21.2 0.0 copy-start.18
  21.2 0.6 copy-done.18
  21.9 0.7 owner_prepare.1
  22.6 7.7 %all-to-all-done = f32[64,1,128]{2,1,0:T(1,128)S(1)} async-done(((f32[64,1,128]{2,1,0:T(1,128)}), f32[64,1,128]{2,1,0:T(1,128)S(1)}, u32[]{:S(2)}, u32[]{:S(2)}) %all-to-all-start) | async-done | bytes 32800 | tf_op jit(solution)/shard_map/all_to_all | solution.py:324
  30.3 1.6 %owner_gather.1 = (bf16[512,1024]{1,0:T(8,128)(2,1)}, bf16[512,128]{1,0:T(8,128)(2,1)S(1)}) custom-call(f32[64,128]{1,0:T(8,128)S(1)} %bitcast.12, f32[512,128]{1,0:T(8,128)S(1)} %get-tuple-element.24.mask_ref, bf16[128,1024]{1,0:T(8,128)(2,1)S(1)} %get-tuple-element.25.kv_ref), custom_call_target="tpu_custom_call" | custom-call | tf_op jit(solution)/shard_map/owner_gather/pallas_call | solution.py:339
  31.8 0.0 copy-start.14
  31.8 0.7 copy-done.14
  32.5 4.7 %all-to-all-start.1 = ((bf16[64,8,1024]{2,1,0:T(8,128)(2,1)}), bf16[64,8,1024]{2,1,0:T(8,128)(2,1)S(1)}, u32[]{:S(2)}, u32[]{:S(2)}) async-start(bf16[64,8,1024]{2,1,0:T(8,128)(2,1)} %bitcast.3), calls=%async_computation.1 | async-start | bytes 2097152 | tf_op jit(solution)/shard_map/all_to_all | solution.py:319
  37.1 0.0 copy-done.12
  37.2 0.0 copy-done.17
  37.2 0.0 copy-start.2
  37.2 1.2 %copy-done.2 = bf16[128,4096]{1,0:T(8,128)(2,1)S(1)} copy-done((bf16[128,4096]{1,0:T(8,128)(2,1)S(1)}, bf16[128,4096]{1,0:T(8,128)(2,1)}, u32[]{:S(2)}) %copy-start.2) | copy-done | bytes 1048600
  38.4 0.0 copy-start.3
  38.4 1.2 %copy-done.3 = bf16[128,4096]{1,0:T(8,128)(2,1)S(1)} copy-done((bf16[128,4096]{1,0:T(8,128)(2,1)S(1)}, bf16[128,4096]{1,0:T(8,128)(2,1)}, u32[]{:S(2)}) %copy-start.3) | copy-done | bytes 1048600
  39.6 0.0 copy-start.13
  39.6 0.9 copy-done.13
  40.5 1.2 %attend_prepare.1 = (bf16[512,256]{1,0:T(8,128)(2,1)S(1)}, bf16[8,512,128]{2,1,0:T(8,128)(2,1)S(1)}, bf16[8,512,128]{2,1,0:T(8,128)(2,1)S(1)}, f32[8,64,512]{2,1,0:T(8,128)S(1)}, f32[8,64,512]{2,1,0:T(8,128)S(1)}) custom-call(s32[2,32]{1,0:T(2,128)S(1)} %copy-done.17, bf16[128,4096]{1,0:T(8,128)(2,1)S(1)} %copy-done.2, bf16[128,4096]{1,0:T(8,128)(2,1)S(1)} %copy-done.3, ...), custom_call_target="tpu_custom_call" | custom-call | flops 134217728 | bytes 7340032 | tf_op jit(solution)/shard_map/attend_prepare/pallas_call | solution.py:347
  41.8 0.0 copy-start.4
  41.8 1.0 copy-done.4
  42.8 0.0 copy-start.6
  42.8 1.0 copy-done.6
  43.7 19.1 %all-to-all-done.1 = bf16[64,8,1024]{2,1,0:T(8,128)(2,1)S(1)} async-done(((bf16[64,8,1024]{2,1,0:T(8,128)(2,1)}), bf16[64,8,1024]{2,1,0:T(8,128)(2,1)S(1)}, u32[]{:S(2)}, u32[]{:S(2)}) %all-to-all-start.1) | async-done | bytes 1048608 | tf_op jit(solution)/shard_map/all_to_all | solution.py:319
  62.8 0.0 copy-start.5
  62.8 1.2 %copy-done.5 = f32[8,64,512]{2,1,0:T(8,128)S(1)} copy-done((f32[8,64,512]{2,1,0:T(8,128)S(1)}, f32[8,64,512]{2,1,0:T(8,128)}, u32[]{:S(2)}) %copy-start.5) | copy-done | bytes 1048600
  64.1 0.0 copy-start.7
  64.1 1.2 %copy-done.7 = f32[8,64,512]{2,1,0:T(8,128)S(1)} copy-done((f32[8,64,512]{2,1,0:T(8,128)S(1)}, f32[8,64,512]{2,1,0:T(8,128)}, u32[]{:S(2)}) %copy-start.7) | copy-done | bytes 1048600
  65.3 3.9 %attend.1 = (bf16[512,1024]{1,0:T(8,128)(2,1)S(1)}, bf16[256,1024]{1,0:T(8,128)(2,1)S(1)}, bf16[8,192,512]{2,1,0:T(8,128)(2,1)S(1)}, bf16[8,64,512]{2,1,0:T(8,128)(2,1)S(1)}) custom-call(bf16[512,256]{1,0:T(8,128)(2,1)S(1)} %get-tuple-element.23.place_ref, bf16[512,1024]{1,0:T(8,128)(2,1)S(1)} %bitcast.10, ...), custom_call_target="tpu_custom_call" | custom-call | tf_op jit(solution)/shard_map/attend/pallas_call | solution.py:360
  69.2 0.0 copy-start.8
  69.2 0.8 copy-done.8
  70.0 0.0 copy-start
  70.0 0.0 copy-start.10
  70.0 0.0 copy-start.15
  70.0 0.0 copy-start.9
  70.0 34.1 %all_to_all.20 = bf16[64,8,1024]{2,1,0:T(8,128)(2,1)S(1)} all-to-all(bf16[64,8,1024]{2,1,0:T(8,128)(2,1)S(1)} %bitcast.11), channel_id=1, replica_groups=mesh['pas'=64,'qry'=8] {'pas'}, dimensions={0} | all-to-all | bytes 2097152 | tf_op jit(solution)/shard_map/all_to_all | solution.py:319
  104.1 0.0 copy-done.15
  104.1 1.0 owner_sum.1
  105.1 0.0 copy-done
  105.1 0.0 copy-done.10
  105.1 9.2 %all-to-all-start.3 = ((bf16[8,8,1024]{2,1,0:T(8,128)(2,1)}), bf16[8,8,1024]{2,1,0:T(8,128)(2,1)S(1)}, u32[]{:S(2)}, u32[]{:S(2)}) async-start(bf16[8,8,1024]{2,1,0:T(8,128)(2,1)} %bitcast.7), calls=%async_computation.3 | async-start | bytes 262144 | tf_op jit(solution)/shard_map/all_to_all | solution.py:385
  114.3 0.0 copy-done.9
  114.3 0.0 copy-start.1
  114.3 1.4 %copy-done.1 = bf16[8,192,512]{2,1,0:T(8,128)(2,1)S(1)} copy-done((bf16[8,192,512]{2,1,0:T(8,128)(2,1)S(1)}, bf16[8,192,512]{2,1,0:T(8,128)(2,1)}, u32[]{:S(2)}) %copy-start.1) | copy-done | bytes 1572888
  115.7 0.0 copy-start.11
  115.7 1.0 copy-done.11
  116.8 2.0 %attend_rest.1 = (bf16[128,4096]{1,0:T(8,128)(2,1)}, bf16[128,512]{1,0:T(8,128)(2,1)}, bf16[128,512]{1,0:T(8,128)(2,1)}) custom-call(bf16[256,1024]{1,0:T(8,128)(2,1)S(1)} %copy-done.9, bf16[8,192,512]{2,1,0:T(8,128)(2,1)S(1)} %copy-done.1, bf16[8,64,512]{2,1,0:T(8,128)(2,1)S(1)} %copy-done.11, bf16[8,512,128]{2,1,0:T(8,128)(2,1)S(1)} %get-tuple-element.27.qh_ref, ...), custom_call_target="tpu_custom_call" | custom-call | flops 805306368 | bytes 6291456 | tf_op jit(solution)/shard_map/attend_rest/pallas_call | solution.py:374
  118.8 0.8 all-to-all-done.3.parts_ref
  119.6 0.6 final_sum.1
Async XLA Ops:
  0.6 36.5 %copy-start.12 = (bf16[128,512]{1,0:T(8,128)(2,1)S(1)}, bf16[128,512]{1,0:T(8,128)(2,1)}, u32[]{:S(2)}) copy-start(bf16[128,512]{1,0:T(8,128)(2,1)} %sk_ref.3) | copy-start | bytes 393220
  0.6 0.7 copy-start.16
  1.4 35.8 %copy-start.17 = (s32[2,32]{1,0:T(2,128)S(1)}, s32[2,32]{1,0:T(2,128)}, u32[]{:S(2)}) copy-start(s32[2,32]{1,0:T(2,128)} %ids_ref.3) | copy-start | bytes 772
  2.3 27.9 %all-to-all-start = ((f32[64,1,128]{2,1,0:T(1,128)}), f32[64,1,128]{2,1,0:T(1,128)S(1)}, u32[]{:S(2)}, u32[]{:S(2)}) async-start(f32[64,1,128]{2,1,0:T(1,128)} %bitcast.1), calls=%async_computation | async-start | bytes 65536 | tf_op jit(solution)/shard_map/all_to_all | solution.py:324
  21.2 0.7 copy-start.18
  31.8 0.7 copy-start.14
  32.5 30.4 %all-to-all-start.1 = ((bf16[64,8,1024]{2,1,0:T(8,128)(2,1)}), bf16[64,8,1024]{2,1,0:T(8,128)(2,1)S(1)}, u32[]{:S(2)}, u32[]{:S(2)}) async-start(bf16[64,8,1024]{2,1,0:T(8,128)(2,1)} %bitcast.3), calls=%async_computation.1 | async-start | bytes 2097152 | tf_op jit(solution)/shard_map/all_to_all | solution.py:319
  37.2 1.2 %copy-start.2 = (bf16[128,4096]{1,0:T(8,128)(2,1)S(1)}, bf16[128,4096]{1,0:T(8,128)(2,1)}, u32[]{:S(2)}) copy-start(bf16[128,4096]{1,0:T(8,128)(2,1)} %q_ref.1) | copy-start | bytes 3145732
  38.4 1.2 %copy-start.3 = (bf16[128,4096]{1,0:T(8,128)(2,1)S(1)}, bf16[128,4096]{1,0:T(8,128)(2,1)}, u32[]{:S(2)}) copy-start(bf16[128,4096]{1,0:T(8,128)(2,1)} %g_ref.1) | copy-start | bytes 3145732
  39.6 0.9 copy-start.13
  41.8 1.0 copy-start.4
  42.8 1.0 copy-start.6
  62.8 1.2 %copy-start.5 = (f32[8,64,512]{2,1,0:T(8,128)S(1)}, f32[8,64,512]{2,1,0:T(8,128)}, u32[]{:S(2)}) copy-start(f32[8,64,512]{2,1,0:T(8,128)} %copy-done.4) | copy-start | bytes 3145732
  64.1 1.2 %copy-start.7 = (f32[8,64,512]{2,1,0:T(8,128)S(1)}, f32[8,64,512]{2,1,0:T(8,128)}, u32[]{:S(2)}) copy-start(f32[8,64,512]{2,1,0:T(8,128)} %copy-done.6) | copy-start | bytes 3145732
  69.2 0.8 copy-start.8
  70.0 35.1 %copy-start = (bf16[8,192,512]{2,1,0:T(8,128)(2,1)}, bf16[8,192,512]{2,1,0:T(8,128)(2,1)S(1)}, u32[]{:S(2)}) copy-start(bf16[8,192,512]{2,1,0:T(8,128)(2,1)S(1)} %get-tuple-element.32.ds_ref) | copy-start | bytes 4718596
  70.0 35.1 %copy-start.10 = (bf16[8,64,512]{2,1,0:T(8,128)(2,1)}, bf16[8,64,512]{2,1,0:T(8,128)(2,1)S(1)}, u32[]{:S(2)}) copy-start(bf16[8,64,512]{2,1,0:T(8,128)(2,1)S(1)} %get-tuple-element.33.w_ref) | copy-start | bytes 1572868
  70.0 34.1 %copy-start.15 = (bf16[512,128]{1,0:T(8,128)(2,1)S(1)}, bf16[512,128]{1,0:T(8,128)(2,1)}, u32[]{:S(2)}) copy-start(bf16[512,128]{1,0:T(8,128)(2,1)} %copy-done.14) | copy-start | bytes 393220
  70.0 44.3 %copy-start.9 = (bf16[256,1024]{1,0:T(8,128)(2,1)S(1)}, bf16[256,1024]{1,0:T(8,128)(2,1)}, u32[]{:S(2)}) copy-start(bf16[256,1024]{1,0:T(8,128)(2,1)} %copy-done.8) | copy-start | bytes 1572868
  105.1 14.5 %all-to-all-start.3 = ((bf16[8,8,1024]{2,1,0:T(8,128)(2,1)}), bf16[8,8,1024]{2,1,0:T(8,128)(2,1)S(1)}, u32[]{:S(2)}, u32[]{:S(2)}) async-start(bf16[8,8,1024]{2,1,0:T(8,128)(2,1)} %bitcast.7), calls=%async_computation.3 | async-start | bytes 262144 | tf_op jit(solution)/shard_map/all_to_all | solution.py:385
  114.3 1.4 %copy-start.1 = (bf16[8,192,512]{2,1,0:T(8,128)(2,1)S(1)}, bf16[8,192,512]{2,1,0:T(8,128)(2,1)}, u32[]{:S(2)}) copy-start(bf16[8,192,512]{2,1,0:T(8,128)(2,1)} %copy-done) | copy-start | bytes 4718596
  115.7 1.0 copy-start.11

commit v3 on v1

v3 whole, which is shorter than its diff:
```python
import functools
import math

import jax
import jax.numpy as jnp
from jax import lax
from jax.experimental import pallas as pl
from jax.experimental.pallas import tpu as pltpu
from jax.sharding import PartitionSpec as P

HQ = 32
HD = 128
Q_LEN = 64
CAP = 2
DEAD = 16.0
NEG = -1e30
SCALE = 1.0 / math.sqrt(HD)
SCALE2 = SCALE * math.log2(math.e)
BF = jnp.bfloat16
F32 = jnp.float32


def iota(shape, dim):
    return lax.broadcasted_iota(jnp.int32, shape, dim)


def dot(a, b, ca=1, cb=0):
    return lax.dot_general(a, b, (((ca,), (cb,)), ((), ())), preferred_element_type=F32)


def one(mask, dtype=BF):
    return jnp.where(mask, 1.0, 0.0).astype(dtype)


def slot_masks(ids, owners, n_local, plen):
    n_query, n_ret = ids.shape
    lanes = n_ret * plen
    own = lax.div(ids, n_local)
    loc = ids - own * n_local
    spread = one(iota((n_ret, lanes), 1) // plen == iota((n_ret, lanes), 0), F32)
    if plen > 1:
        own = dot(own.astype(F32), spread).astype(jnp.int32)
        loc = dot(loc.astype(F32), spread)
    else:
        loc = loc.astype(F32)
    before = one(
        (iota((lanes, lanes), 0) % plen == 0)
        & (iota((lanes, lanes), 0) // plen < iota((lanes, lanes), 1) // plen)
    )
    heads = one(iota((lanes, lanes), 0) % plen == 0)
    masks = []
    locals_ = []
    used = None
    for n in range(n_query):
        hit = iota((owners, lanes), 0) == own[n : n + 1]
        hit_b = one(hit)
        rank = dot(hit_b, before)
        if used is not None:
            rank = rank + used
        total = dot(hit_b, heads)
        used = total if used is None else used + total
        masks.append([one(hit & (rank == float(c)), F32) for c in range(CAP)])
        locals_.append(loc[n : n + 1])
    return masks, locals_


def request_kernel(owners, n_local, plen, ids_ref, req_ref):
    masks, locs = slot_masks(ids_ref[...], owners, n_local, 1)
    wanted = []
    for c in range(CAP):
        total = 0.0
        for mask, loc in zip(masks, locs):
            total = total + mask[c] * (loc + 1.0)
        wanted.append(jnp.sum(total, axis=1, keepdims=True))
    width = CAP * n_local * plen
    lane = iota((owners, width), 1)
    slot = lane // (n_local * plen)
    local = (lane % (n_local * plen)) // plen
    picked = jnp.where(slot == 0, wanted[0], wanted[1])
    req_ref[...] = one(picked == (local + 1).astype(F32), F32)


def prepare_kernel(
    owners,
    n_local,
    plen,
    len_ref,
    pk_ref,
    pv_ref,
    ids_ref,
    mask_ref,
    kv_ref,
    place_ref,
):
    rows = owners * CAP * plen
    width = CAP * n_local * plen
    chunk = CAP * plen
    row = iota((rows, width), 0)
    lane = iota((rows, width), 1)
    same = ((row % chunk) // plen == lane // (n_local * plen)) & (row % plen == lane % plen)
    lane_row = iota((1, width), 1)
    lane_m = (lane_row % (n_local * plen)) // plen
    live = jnp.zeros((1, width), jnp.int32)
    for m in range(n_local):
        live = jnp.where(lane_m == m, len_ref[m], live)
    live = lane_row % plen < live
    mask_ref[...] = one(same & live)
    kv_width = pk_ref.shape[2]
    half = n_local * plen
    for c in range(CAP):
        for m in range(n_local):
            at = c * half + m * plen
            kv_ref[at : at + plen, :kv_width] = pk_ref[m]
            kv_ref[at : at + plen, kv_width:] = pv_ref[m]

    n_query, n_ret = ids_ref.shape
    lanes = n_ret * plen
    masks, _ = slot_masks(ids_ref[...], owners, n_local, plen)
    row = iota((rows, CAP * owners), 0)
    lane = iota((rows, CAP * owners), 1)
    who = one((row // chunk == lane % owners) & ((row % chunk) // plen == lane // owners))
    same = iota((rows, lanes), 0) % plen == iota((rows, lanes), 1) % plen
    for n in range(n_query):
        asked = jnp.concatenate([m.astype(BF) for m in masks[n]], axis=0)
        place_ref[:, n * lanes : (n + 1) * lanes] = jnp.where(same, dot(who, asked), 0.0).astype(BF)


def owner_kernel(owners, plen, req_ref, mask_ref, kv_ref, send_ref, table_ref):
    rows, width = mask_ref.shape
    chunk = CAP * plen
    who = one(iota((rows, owners), 0) // chunk == iota((rows, owners), 1))
    spread = dot(who, req_ref[...].astype(BF))
    table = (spread * mask_ref[...].astype(F32)).astype(BF)
    table_ref[...] = table
    alive = dot(table, jnp.ones((width, HD), BF))
    fill = (1.0 - alive) * DEAD
    kv_width = kv_ref.shape[1] // 2
    sent = dot(table, kv_ref[...])
    for g in range(kv_width // HD):
        send_ref[:, g * HD : (g + 1) * HD] = (sent[:, g * HD : (g + 1) * HD] + fill).astype(BF)
    send_ref[:, kv_width:] = sent[:, kv_width:].astype(BF)


def attend_kernel(
    place_ref,
    recv_ref,
    q_ref,
    g_ref,
    sk_ref,
    sv_ref,
    dq_ref,
    dsk_ref,
    dsv_ref,
    terms_ref,
    kv_ref,
    out_ref,
):
    kv_width = sk_ref.shape[1]
    kv_heads = kv_width // HD
    group = HQ // kv_heads
    q_len = Q_LEN
    n_query = sk_ref.shape[0] // q_len
    lanes = place_ref.shape[1] // n_query
    wide = group * q_len
    kv_ref[...] = dot(place_ref[...], recv_ref[...], 0, 0).astype(BF)
    causal = iota((q_len, wide), 0) <= iota((q_len, wide), 1) % q_len
    for n in range(n_query):
        r0 = n * q_len
        k0 = n * lanes
        for g in range(kv_heads):
            col = g * HD
            vcol = kv_width + g * HD
            heads = [slice((g * group + x) * HD, (g * group + x + 1) * HD) for x in range(group)]
            q = jnp.concatenate([q_ref[r0 : r0 + q_len, h] for h in heads], axis=0)
            go = jnp.concatenate([g_ref[r0 : r0 + q_len, h] for h in heads], axis=0)
            pk = kv_ref[k0 : k0 + lanes, col : col + HD]
            keys = jnp.concatenate([pk, sk_ref[r0 : r0 + q_len, col : col + HD]], axis=0)
            values = jnp.concatenate(
                [kv_ref[k0 : k0 + lanes, vcol : vcol + HD], sv_ref[r0 : r0 + q_len, col : col + HD]],
                axis=0,
            )
            alive = pk.astype(F32) < 0.5 * DEAD
            alive = jnp.concatenate([alive] * (wide // HD), axis=1)
            s = dot(keys, q, 1, 1) * SCALE2
            s = jnp.concatenate(
                [jnp.where(alive, s[:lanes], NEG), jnp.where(causal, s[lanes:], NEG)], axis=0
            )
            e = jnp.exp2(s - jnp.max(s, axis=0, keepdims=True))
            p = e * (1.0 / jnp.sum(e, axis=0, keepdims=True))
            w = p.astype(BF)
            dp = dot(values, go, 1, 1)
            delta = jnp.sum(w.astype(F32) * dp, axis=0, keepdims=True)
            ds = (p * (dp - delta)).astype(BF)
            dv = dot(w, go)
            dk = dot(ds, q) * SCALE
            dq = (dot(ds, keys, 0, 0) * SCALE).astype(BF)
            for x in range(group):
                at_col = (g * group + x) * HD
                dq_ref[r0 : r0 + q_len, at_col : at_col + HD] = dq[x * q_len : (x + 1) * q_len]
            dsk_ref[r0 : r0 + q_len, col : col + HD] = dk[lanes:].astype(BF)
            dsv_ref[r0 : r0 + q_len, col : col + HD] = dv[lanes:].astype(BF)
            out_ref[k0 : k0 + lanes, col : col + HD] = dk[:lanes].astype(BF)
            out_ref[k0 : k0 + lanes, vcol : vcol + HD] = dv[:lanes].astype(BF)
    terms_ref[...] = dot(place_ref[...], out_ref[...]).astype(BF)


def owner_sum_kernel(table_ref, back_ref, sum_ref):
    total = dot(table_ref[...], back_ref[...], 0, 0)
    half = total.shape[0] // CAP
    sum_ref[...] = (total[:half] + total[half:]).astype(BF)


def final_kernel(parts_ref, gk_ref, gv_ref):
    total = jnp.sum(parts_ref[...].astype(F32), axis=0).astype(BF)
    n_out, plen, kv_width = gk_ref.shape
    for m in range(n_out):
        gk_ref[m] = total[m * plen : (m + 1) * plen, :kv_width]
        gv_ref[m] = total[m * plen : (m + 1) * plen, kv_width:]


VMEM = pl.BlockSpec(memory_space=pltpu.VMEM)
SMEM = pl.BlockSpec(memory_space=pltpu.SMEM)


def call(kernel, out_shape, in_specs, name, limit=16, scratch=(), cost=None):
    several = isinstance(out_shape, (list, tuple))
    return pl.pallas_call(
        kernel,
        out_shape=out_shape,
        in_specs=in_specs,
        out_specs=[VMEM] * len(out_shape) if several else VMEM,
        scratch_shapes=list(scratch),
        compiler_params=pltpu.CompilerParams(vmem_limit_bytes=limit * 2**20),
        cost_estimate=cost,
        name=name,
    )


def cost(flops, mib, exps=0):
    return pl.CostEstimate(
        flops=int(flops), bytes_accessed=int(mib * 2**20), transcendentals=int(exps)
    )


def on_device(
    queries,
    grad_out,
    suffix_keys,
    suffix_values,
    passage_keys,
    passage_values,
    passage_lengths,
    retrieved,
):
    owners = lax.axis_size("pas")
    groups = lax.axis_size("qry")
    n_local, plen, kv_width = passage_keys.shape
    n_query, n_ret = retrieved.shape
    lanes = n_ret * plen
    rows = owners * CAP * plen
    width = CAP * n_local * plen
    sds = jax.ShapeDtypeStruct
    dims = (owners, n_local, plen)

    def exchange(x):
        parts = x.reshape((owners, rows // owners, x.shape[1]))
        return lax.all_to_all(parts, "pas", split_axis=0, concat_axis=0, tiled=True).reshape(x.shape)

    request = call(
        functools.partial(request_kernel, *dims), sds((owners, width), F32), [VMEM], "request"
    )(retrieved)
    asked = lax.all_to_all(
        request.reshape(owners, 1, width), "pas", split_axis=0, concat_axis=0, tiled=True
    ).reshape(owners, width)

    mask, tables, place = call(
        functools.partial(prepare_kernel, *dims),
        [
            sds((rows, width), BF),
            sds((width, 2 * kv_width), BF),
            sds((rows, n_query * lanes), BF),
        ],
        [SMEM] + [VMEM] * 3,
        "prepare",
        cost=cost(1e8, 1),
    )(passage_lengths, passage_keys, passage_values, retrieved)
    send, table = call(
        functools.partial(owner_kernel, owners, plen),
        [sds((rows, 2 * kv_width), BF), sds((rows, width), BF)],
        [VMEM, VMEM, VMEM],
        "owner_gather",
    )(asked, mask, tables)
    recv = exchange(send)

    dq, dsk, dsv, terms = call(
        attend_kernel,
        [
            sds(queries.shape, BF),
            sds(suffix_keys.shape, BF),
            sds(suffix_values.shape, BF),
            sds((rows, 2 * kv_width), BF),
        ],
        [VMEM] * 6,
        "attend",
        limit=24,
        scratch=[pltpu.VMEM((n_query * lanes, 2 * kv_width), BF)] * 2,
    )(place, recv, queries, grad_out, suffix_keys, suffix_values)
    back = exchange(terms)

    sums = call(owner_sum_kernel, sds((n_local * plen, 2 * kv_width), BF), [VMEM] * 2, "owner_sum")(
        table, back
    )
    parts = lax.all_to_all(
        sums.reshape(groups, n_local // groups * plen, 2 * kv_width),
        "qry",
        split_axis=0,
        concat_axis=0,
        tiled=True,
    )
    out = sds((n_local // groups, plen, kv_width), BF)
    gk, gv = call(final_kernel, [out, out], [VMEM], "final_sum")(parts)
    return dq, dsk, dsv, gk, gv


def solution(mesh):
    in_specs = (
        P(("pas", "qry"), None),
        P(("pas", "qry"), None),
        P(("pas", "qry"), None),
        P(("pas", "qry"), None),
        P("pas", None, None),
        P("pas", None, None),
        P("pas"),
        P(("pas", "qry"), None),
    )
    out_specs = (
        P(("pas", "qry"), None),
        P(("pas", "qry"), None),
        P(("pas", "qry"), None),
        P(("pas", "qry"), None, None),
        P(("pas", "qry"), None, None),
    )
    return jax.shard_map(
        on_device, mesh=mesh, in_specs=in_specs, out_specs=out_specs, check_vma=False
    )
```

time: 117 us -> 115 us (0.983)
    pallas_call x3 -> x4, Pallas kernels: 7.2 us -> 7.23 us  [the longest x1 4.96 us: on_device(): call(attend_kernel, [sds(queries.shape, BF), sds(suffix_keys.shape, BF),...]
  transfers between devices with their start and end apart: 1 -> 1, of which waited for: 1 -> 1; matrix products, arithmetic and copies ran while one was open for 0% -> 0% of each run, Pallas kernels for 0% -> 1%
where the time goes in v3:
time: 115 us
  blocking collectives  77.9 us (68%)
  starting transfers between devices  17.3 us (15%)
  waiting for transfers between devices  8.84 us (8%)
  Pallas kernels  8.4 us (7%)
  local copies, waits for them, and re-layouts  1.54 us (1%)
    all_to_all x2, blocking collectives, exchange(): lax.all_to_all(parts, 'pas', split_axis=0, concat_axis=0, tiled=True)  63.6 us
    all_to_all x1, starting transfers between devices, on_device(): lax.all_to_all(request.reshape(owners, 1, width), 'pas', split_axis=0, co...  17.3 us
    all_to_all x1, blocking collectives, on_device(): lax.all_to_all(sums.reshape(groups, n_local // groups * plen, 2 * kv_widt...  14.3 us
    all_to_all x1, waiting for transfers between devices, on_device(): lax.all_to_all(request.reshape(owners, 1, width), 'pas', split_axis=0, co...  8.84 us
    pallas_call x1, Pallas kernels, on_device(): call(attend_kernel, [sds(queries.shape, BF), sds(suffix_keys.shape, BF),...  4.96 us
  transfers between devices with their start and end apart: 1, of which 1 were waited for; matrix products, arithmetic and copies ran while one was open for 0% of the time, Pallas kernels for 1%

profile of v3, /device:TPU:1, one launch (start us, length us, event | category | flops | bytes accessed | tf_op | source)
XLA Modules:
  0.0 114.7 jit_solution(3020936694987018059)
XLA Ops:
  0.6 0.0 copy-start.4
  0.6 0.7 copy-done.4
  1.3 0.0 copy-start.6
  1.3 0.8 request.1
  2.2 0.0 copy-start.5
  2.2 0.0 copy-start.8
  2.2 17.3 %all-to-all-start = ((f32[64,1,128]{2,1,0:T(1,128)}), f32[64,1,128]{2,1,0:T(1,128)S(1)}, u32[]{:S(2)}, u32[]{:S(2)}) async-start(f32[64,1,128]{2,1,0:T(1,128)} %bitcast.1), calls=%async_computation | async-start | bytes 65536 | tf_op jit(solution)/shard_map/all_to_all | solution.py:272
  19.4 0.0 copy-done.6
  19.5 0.0 copy-done.5
  19.5 0.0 copy-done.8
  19.5 0.0 copy-start.7
  19.5 0.8 copy-done.7
  20.3 1.0 prepare.1
  21.4 8.8 %all-to-all-done = f32[64,1,128]{2,1,0:T(1,128)S(1)} async-done(((f32[64,1,128]{2,1,0:T(1,128)}), f32[64,1,128]{2,1,0:T(1,128)S(1)}, u32[]{:S(2)}, u32[]{:S(2)}) %all-to-all-start) | async-done | bytes 32800 | tf_op jit(solution)/shard_map/all_to_all | solution.py:272
  30.2 0.0 copy-start.2
  30.2 0.0 copy-start.3
  30.2 0.6 owner_gather.1
  30.8 0.0 copy-start
  30.8 0.0 copy-start.1
  30.8 29.7 %all_to_all.20 = bf16[64,8,1024]{2,1,0:T(8,128)(2,1)S(1)} all-to-all(bf16[64,8,1024]{2,1,0:T(8,128)(2,1)S(1)} %bitcast.12), channel_id=1, replica_groups=mesh['pas'=64,'qry'=8] {'pas'}, dimensions={0} | all-to-all | bytes 2097152 | tf_op jit(solution)/shard_map/all_to_all | solution.py:267
  60.5 0.0 copy-done.2
  60.5 0.0 copy-done.3
  60.5 0.0 copy-done
  60.5 0.0 copy-done.1
  60.5 5.0 %attend.1 = (bf16[128,4096]{1,0:T(8,128)(2,1)}, bf16[128,512]{1,0:T(8,128)(2,1)}, bf16[128,512]{1,0:T(8,128)(2,1)}, bf16[512,1024]{1,0:T(8,128)(2,1)S(1)}) custom-call(bf16[512,256]{1,0:T(8,128)(2,1)S(1)} %get-tuple-element.16.place_ref, bf16[512,1024]{1,0:T(8,128)(2,1)S(1)} %bitcast.9, bf16[128,4096]{1,0:T(8,128)(2,1)S(1)} %copy-done, ...), custom_call_target="tpu_custom_call" | custom-call | tf_op jit(solution)/shard_map/attend/pallas_call | solution.py:295
  65.5 34.0 %all_to_all.21 = bf16[64,8,1024]{2,1,0:T(8,128)(2,1)S(1)} all-to-all(bf16[64,8,1024]{2,1,0:T(8,128)(2,1)S(1)} %bitcast.11), channel_id=1, replica_groups=mesh['pas'=64,'qry'=8] {'pas'}, dimensions={0} | all-to-all | bytes 2097152 | tf_op jit(solution)/shard_map/all_to_all | solution.py:267
  99.4 0.3 owner_sum.1
  99.8 14.3 %all_to_all.22.parts_ref = bf16[8,8,1024]{2,1,0:T(8,128)(2,1)S(1)} all-to-all(bf16[8,8,1024]{2,1,0:T(8,128)(2,1)S(1)} %bitcast.13), channel_id=1, replica_groups=mesh['pas'=64,'qry'=8] {'qry'}, dimensions={0} | all-to-all | bytes 262144 | tf_op jit(solution)/shard_map/all_to_all | solution.py:313
  114.1 0.6 final_sum.1
Async XLA Ops:
  0.6 0.7 copy-start.4
  1.3 18.1 %copy-start.6 = (bf16[16,4,512]{2,1,0:T(4,128)(2,1)S(1)}, bf16[16,4,512]{2,1,0:T(4,128)(2,1)}, u32[]{:S(2)}) copy-start(bf16[16,4,512]{2,1,0:T(4,128)(2,1)} %pk_ref.1) | copy-start | bytes 196612
  2.2 17.3 %copy-start.5 = (s32[2,32]{1,0:T(2,128)S(1)}, s32[2,32]{1,0:T(2,128)}, u32[]{:S(2)}) copy-start(s32[2,32]{1,0:T(2,128)} %ids_ref.3) | copy-start | bytes 772
  2.2 17.3 %copy-start.8 = (s32[16]{0:T(128)S(1)}, s32[16]{0:T(128)}, u32[]{:S(2)}) copy-start(s32[16]{0:T(128)} %len_ref.1) | copy-start | bytes 196
  2.2 28.0 %all-to-all-start = ((f32[64,1,128]{2,1,0:T(1,128)}), f32[64,1,128]{2,1,0:T(1,128)S(1)}, u32[]{:S(2)}, u32[]{:S(2)}) async-start(f32[64,1,128]{2,1,0:T(1,128)} %bitcast.1), calls=%async_computation | async-start | bytes 65536 | tf_op jit(solution)/shard_map/all_to_all | solution.py:272
  19.5 0.8 copy-start.7
  30.2 30.3 %copy-start.2 = (bf16[128,512]{1,0:T(8,128)(2,1)S(1)}, bf16[128,512]{1,0:T(8,128)(2,1)}, u32[]{:S(2)}) copy-start(bf16[128,512]{1,0:T(8,128)(2,1)} %sk_ref.1) | copy-start | bytes 393220
  30.2 30.3 %copy-start.3 = (bf16[128,512]{1,0:T(8,128)(2,1)S(1)}, bf16[128,512]{1,0:T(8,128)(2,1)}, u32[]{:S(2)}) copy-start(bf16[128,512]{1,0:T(8,128)(2,1)} %sv_ref.1) | copy-start | bytes 393220
  30.8 29.7 %copy-start = (bf16[128,4096]{1,0:T(8,128)(2,1)S(1)}, bf16[128,4096]{1,0:T(8,128)(2,1)}, u32[]{:S(2)}) copy-start(bf16[128,4096]{1,0:T(8,128)(2,1)} %q_ref.1) | copy-start | bytes 3145732
  30.8 29.7 %copy-start.1 = (bf16[128,4096]{1,0:T(8,128)(2,1)S(1)}, bf16[128,4096]{1,0:T(8,128)(2,1)}, u32[]{:S(2)}) copy-start(bf16[128,4096]{1,0:T(8,128)(2,1)} %g_ref.1) | copy-start | bytes 3145732

commit v4 on v3

--- a/solution.py
+++ b/solution.py
@@ -32,52 +32,34 @@
     return jnp.where(mask, 1.0, 0.0).astype(dtype)
 
 
-def slot_masks(ids, owners, n_local, plen):
+def slots(ids, owners, n_local, spread):
     n_query, n_ret = ids.shape
-    lanes = n_ret * plen
+    lanes = n_ret * spread
     own = lax.div(ids, n_local)
-    loc = ids - own * n_local
-    spread = one(iota((n_ret, lanes), 1) // plen == iota((n_ret, lanes), 0), F32)
-    if plen > 1:
-        own = dot(own.astype(F32), spread).astype(jnp.int32)
-        loc = dot(loc.astype(F32), spread)
-    else:
-        loc = loc.astype(F32)
-    before = one(
-        (iota((lanes, lanes), 0) % plen == 0)
-        & (iota((lanes, lanes), 0) // plen < iota((lanes, lanes), 1) // plen)
-    )
-    heads = one(iota((lanes, lanes), 0) % plen == 0)
-    masks = []
-    locals_ = []
-    used = None
-    for n in range(n_query):
-        hit = iota((owners, lanes), 0) == own[n : n + 1]
-        hit_b = one(hit)
-        rank = dot(hit_b, before)
-        if used is not None:
-            rank = rank + used
-        total = dot(hit_b, heads)
-        used = total if used is None else used + total
-        masks.append([one(hit & (rank == float(c)), F32) for c in range(CAP)])
-        locals_.append(loc[n : n + 1])
-    return masks, locals_
+    loc = (ids - own * n_local).astype(F32)
+    if spread > 1:
+        copies = one(iota((n_ret, lanes), 1) // spread == iota((n_ret, lanes), 0), F32)
+        own = dot(own.astype(F32), copies).astype(jnp.int32)
+        loc = dot(loc, copies)
+    owner = iota((owners, lanes), 0)
+    hits = [owner == own[n : n + 1] for n in range(n_query)]
+    locs = [loc[n : n + 1] for n in range(n_query)]
+    low = functools.reduce(
+        jnp.minimum, [jnp.where(h, x, float(n_local)) for h, x in zip(hits, locs)]
+    )
+    high = functools.reduce(jnp.maximum, [jnp.where(h, x, -1.0) for h, x in zip(hits, locs)])
+    low = jnp.min(low, axis=1, keepdims=True)
+    high = jnp.max(high, axis=1, keepdims=True)
+    return low, jnp.where(high > low, high, -1.0), hits, locs
 
 
 def request_kernel(owners, n_local, plen, ids_ref, req_ref):
-    masks, locs = slot_masks(ids_ref[...], owners, n_local, 1)
-    wanted = []
-    for c in range(CAP):
-        total = 0.0
-        for mask, loc in zip(masks, locs):
-            total = total + mask[c] * (loc + 1.0)
-        wanted.append(jnp.sum(total, axis=1, keepdims=True))
+    low, high, _, _ = slots(ids_ref[...], owners, n_local, 1)
     width = CAP * n_local * plen
     lane = iota((owners, width), 1)
     slot = lane // (n_local * plen)
     local = (lane % (n_local * plen)) // plen
-    picked = jnp.where(slot == 0, wanted[0], wanted[1])
-    req_ref[...] = one(picked == (local + 1).astype(F32), F32)
+    req_ref[...] = one(jnp.where(slot == 0, low, high) == local.astype(F32), F32)
 
 
 def prepare_kernel(
@@ -115,13 +97,15 @@
 
     n_query, n_ret = ids_ref.shape
     lanes = n_ret * plen
-    masks, _ = slot_masks(ids_ref[...], owners, n_local, plen)
+    low, high, hits, locs = slots(ids_ref[...], owners, n_local, plen)
     row = iota((rows, CAP * owners), 0)
     lane = iota((rows, CAP * owners), 1)
     who = one((row // chunk == lane % owners) & ((row % chunk) // plen == lane // owners))
     same = iota((rows, lanes), 0) % plen == iota((rows, lanes), 1) % plen
     for n in range(n_query):
-        asked = jnp.concatenate([m.astype(BF) for m in masks[n]], axis=0)
+        asked = jnp.concatenate(
+            [one(hits[n] & (locs[n] == picked)) for picked in (low, high)], axis=0
+        )
         place_ref[:, n * lanes : (n + 1) * lanes] = jnp.where(same, dot(who, asked), 0.0).astype(BF)
 
 
@@ -164,43 +148,65 @@
     wide = group * q_len
     kv_ref[...] = dot(place_ref[...], recv_ref[...], 0, 0).astype(BF)
     causal = iota((q_len, wide), 0) <= iota((q_len, wide), 1) % q_len
-    for n in range(n_query):
+    pairs = [(n, g) for n in range(n_query) for g in range(kv_heads)]
+
+    def load(n, g):
         r0 = n * q_len
         k0 = n * lanes
-        for g in range(kv_heads):
-            col = g * HD
-            vcol = kv_width + g * HD
-            heads = [slice((g * group + x) * HD, (g * group + x + 1) * HD) for x in range(group)]
-            q = jnp.concatenate([q_ref[r0 : r0 + q_len, h] for h in heads], axis=0)
-            go = jnp.concatenate([g_ref[r0 : r0 + q_len, h] for h in heads], axis=0)
-            pk = kv_ref[k0 : k0 + lanes, col : col + HD]
-            keys = jnp.concatenate([pk, sk_ref[r0 : r0 + q_len, col : col + HD]], axis=0)
-            values = jnp.concatenate(
-                [kv_ref[k0 : k0 + lanes, vcol : vcol + HD], sv_ref[r0 : r0 + q_len, col : col + HD]],
-                axis=0,
-            )
-            alive = pk.astype(F32) < 0.5 * DEAD
-            alive = jnp.concatenate([alive] * (wide // HD), axis=1)
-            s = dot(keys, q, 1, 1) * SCALE2
-            s = jnp.concatenate(
-                [jnp.where(alive, s[:lanes], NEG), jnp.where(causal, s[lanes:], NEG)], axis=0
-            )
-            e = jnp.exp2(s - jnp.max(s, axis=0, keepdims=True))
-            p = e * (1.0 / jnp.sum(e, axis=0, keepdims=True))
-            w = p.astype(BF)
-            dp = dot(values, go, 1, 1)
-            delta = jnp.sum(w.astype(F32) * dp, axis=0, keepdims=True)
-            ds = (p * (dp - delta)).astype(BF)
-            dv = dot(w, go)
-            dk = dot(ds, q) * SCALE
-            dq = (dot(ds, keys, 0, 0) * SCALE).astype(BF)
-            for x in range(group):
-                at_col = (g * group + x) * HD
-                dq_ref[r0 : r0 + q_len, at_col : at_col + HD] = dq[x * q_len : (x + 1) * q_len]
-            dsk_ref[r0 : r0 + q_len, col : col + HD] = dk[lanes:].astype(BF)
-            dsv_ref[r0 : r0 + q_len, col : col + HD] = dv[lanes:].astype(BF)
-            out_ref[k0 : k0 + lanes, col : col + HD] = dk[:lanes].astype(BF)
-            out_ref[k0 : k0 + lanes, vcol : vcol + HD] = dv[:lanes].astype(BF)
+        col = slice(g * HD, (g + 1) * HD)
+        vcol = slice(kv_width + g * HD, kv_width + (g + 1) * HD)
+        heads = [slice((g * group + x) * HD, (g * group + x + 1) * HD) for x in range(group)]
+        q = jnp.concatenate([q_ref[r0 : r0 + q_len, h] for h in heads], axis=0)
+        go = jnp.concatenate([g_ref[r0 : r0 + q_len, h] for h in heads], axis=0)
+        keys = jnp.concatenate(
+            [kv_ref[k0 : k0 + lanes, col], sk_ref[r0 : r0 + q_len, col]], axis=0
+        )
+        values = jnp.concatenate(
+            [kv_ref[k0 : k0 + lanes, vcol], sv_ref[r0 : r0 + q_len, col]], axis=0
+        )
+        return q, go, keys, values
+
+    def products(n, g):
+        q, go, keys, values = load(n, g)
+        return dot(keys, q, 1, 1), dot(values, go, 1, 1)
+
+    def weigh(n, g, s, dp):
+        pk = kv_ref[n * lanes : (n + 1) * lanes, g * HD : (g + 1) * HD]
+        alive = pk.astype(F32) < 0.5 * DEAD
+        alive = jnp.concatenate([alive] * (wide // HD), axis=1)
+        s = s * SCALE2
+        s = jnp.concatenate(
+            [jnp.where(alive, s[:lanes], NEG), jnp.where(causal, s[lanes:], NEG)], axis=0
+        )
+        e = jnp.exp2(s - jnp.max(s, axis=0, keepdims=True))
+        p = e * (1.0 / jnp.sum(e, axis=0, keepdims=True))
+        w = p.astype(BF)
+        delta = jnp.sum(w.astype(F32) * dp, axis=0, keepdims=True)
+        return w, (p * (dp - delta)).astype(BF)
+
+    def store(n, g, w, ds):
+        q, go, keys, _ = load(n, g)
+        r0 = n * q_len
+        k0 = n * lanes
+        col = slice(g * HD, (g + 1) * HD)
+        vcol = slice(kv_width + g * HD, kv_width + (g + 1) * HD)
+        dv = dot(w, go)
+        dk = dot(ds, q) * SCALE
+        dq = (dot(ds, keys, 0, 0) * SCALE).astype(BF)
+        for x in range(group):
+            at = (g * group + x) * HD
+            dq_ref[r0 : r0 + q_len, at : at + HD] = dq[x * q_len : (x + 1) * q_len]
+        dsk_ref[r0 : r0 + q_len, col] = dk[lanes:].astype(BF)
+        dsv_ref[r0 : r0 + q_len, col] = dv[lanes:].astype(BF)
+        out_ref[k0 : k0 + lanes, col] = dk[:lanes].astype(BF)
+        out_ref[k0 : k0 + lanes, vcol] = dv[:lanes].astype(BF)
+
+    for a in range(0, len(pairs), 2):
+        two = pairs[a : a + 2]
+        both = [products(*pair) for pair in two]
+        both = [weigh(*pair, *x) for pair, x in zip(two, both)]
+        for pair, x in zip(two, both):
+            store(*pair, *x)
     terms_ref[...] = dot(place_ref[...], out_ref[...]).astype(BF)
 
 

time: 115 us -> 114 us (level)
  no operation moved by 1% of the time
where the time goes in v4:
time: 114 us
  blocking collectives  78 us (68%)
  starting transfers between devices  17.3 us (15%)
  waiting for transfers between devices  8.89 us (8%)
  Pallas kernels  7.74 us (7%)
  local copies, waits for them, and re-layouts  1.54 us (1%)
    all_to_all x2, blocking collectives, exchange(): lax.all_to_all(parts, 'pas', split_axis=0, concat_axis=0, tiled=True)  63.6 us
    all_to_all x1, starting transfers between devices, on_device(): lax.all_to_all(request.reshape(owners, 1, width), 'pas', split_axis=0, co...  17.3 us
    all_to_all x1, blocking collectives, on_device(): lax.all_to_all(sums.reshape(groups, n_local // groups * plen, 2 * kv_widt...  14.4 us
    all_to_all x1, waiting for transfers between devices, on_device(): lax.all_to_all(request.reshape(owners, 1, width), 'pas', split_axis=0, co...  8.89 us
    pallas_call x1, Pallas kernels, on_device(): call(attend_kernel, [sds(queries.shape, BF), sds(suffix_keys.shape, BF),...  4.47 us
  transfers between devices with their start and end apart: 1, of which 1 were waited for; matrix products, arithmetic and copies ran while one was open for 0% of the time, Pallas kernels for 1%

profile of v4, /device:TPU:1, one launch (start us, length us, event | category | flops | bytes accessed | tf_op | source)
XLA Modules:
  0.0 114.1 jit_solution(14159581818870105699)
XLA Ops:
  0.6 0.0 copy-start.4
  0.6 0.7 copy-done.4
  1.3 0.0 copy-start.6
  1.3 0.7 request.1
  2.0 0.0 copy-start.5
  2.0 0.0 copy-start.8
  2.0 17.3 %all-to-all-start = ((f32[64,1,128]{2,1,0:T(1,128)}), f32[64,1,128]{2,1,0:T(1,128)S(1)}, u32[]{:S(2)}, u32[]{:S(2)}) async-start(f32[64,1,128]{2,1,0:T(1,128)} %bitcast.1), calls=%async_computation | async-start | bytes 65536 | tf_op jit(solution)/shard_map/all_to_all | solution.py:278
  19.3 0.0 copy-done.6
  19.3 0.0 copy-done.5
  19.3 0.0 copy-done.8
  19.3 0.0 copy-start.7
  19.4 0.8 copy-done.7
  20.2 1.0 prepare.1
  21.2 8.9 %all-to-all-done = f32[64,1,128]{2,1,0:T(1,128)S(1)} async-done(((f32[64,1,128]{2,1,0:T(1,128)}), f32[64,1,128]{2,1,0:T(1,128)S(1)}, u32[]{:S(2)}, u32[]{:S(2)}) %all-to-all-start) | async-done | bytes 32800 | tf_op jit(solution)/shard_map/all_to_all | solution.py:278
  30.1 0.0 copy-start.2
  30.1 0.0 copy-start.3
  30.1 0.6 owner_gather.1
  30.7 0.0 copy-start
  30.7 0.0 copy-start.1
  30.7 29.7 %all_to_all.20 = bf16[64,8,1024]{2,1,0:T(8,128)(2,1)S(1)} all-to-all(bf16[64,8,1024]{2,1,0:T(8,128)(2,1)S(1)} %bitcast.12), channel_id=1, replica_groups=mesh['pas'=64,'qry'=8] {'pas'}, dimensions={0} | all-to-all | bytes 2097152 | tf_op jit(solution)/shard_map/all_to_all | solution.py:273
  60.4 0.0 copy-done.2
  60.4 0.0 copy-done.3
  60.4 0.0 copy-done
  60.4 0.0 copy-done.1
  60.4 4.5 %attend.1 = (bf16[128,4096]{1,0:T(8,128)(2,1)}, bf16[128,512]{1,0:T(8,128)(2,1)}, bf16[128,512]{1,0:T(8,128)(2,1)}, bf16[512,1024]{1,0:T(8,128)(2,1)S(1)}) custom-call(bf16[512,256]{1,0:T(8,128)(2,1)S(1)} %get-tuple-element.16.place_ref, bf16[512,1024]{1,0:T(8,128)(2,1)S(1)} %bitcast.9, bf16[128,4096]{1,0:T(8,128)(2,1)S(1)} %copy-done, ...), custom_call_target="tpu_custom_call" | custom-call | tf_op jit(solution)/shard_map/attend/pallas_call | solution.py:301
  64.9 33.9 %all_to_all.21 = bf16[64,8,1024]{2,1,0:T(8,128)(2,1)S(1)} all-to-all(bf16[64,8,1024]{2,1,0:T(8,128)(2,1)S(1)} %bitcast.11), channel_id=1, replica_groups=mesh['pas'=64,'qry'=8] {'pas'}, dimensions={0} | all-to-all | bytes 2097152 | tf_op jit(solution)/shard_map/all_to_all | solution.py:273
  98.8 0.3 owner_sum.1
  99.1 14.4 %all_to_all.22.parts_ref = bf16[8,8,1024]{2,1,0:T(8,128)(2,1)S(1)} all-to-all(bf16[8,8,1024]{2,1,0:T(8,128)(2,1)S(1)} %bitcast.13), channel_id=1, replica_groups=mesh['pas'=64,'qry'=8] {'qry'}, dimensions={0} | all-to-all | bytes 262144 | tf_op jit(solution)/shard_map/all_to_all | solution.py:319
  113.5 0.6 final_sum.1
Async XLA Ops:
  0.6 0.7 copy-start.4
  1.3 18.0 %copy-start.6 = (bf16[16,4,512]{2,1,0:T(4,128)(2,1)S(1)}, bf16[16,4,512]{2,1,0:T(4,128)(2,1)}, u32[]{:S(2)}) copy-start(bf16[16,4,512]{2,1,0:T(4,128)(2,1)} %pk_ref.1) | copy-start | bytes 196612
  2.0 17.3 %copy-start.5 = (s32[2,32]{1,0:T(2,128)S(1)}, s32[2,32]{1,0:T(2,128)}, u32[]{:S(2)}) copy-start(s32[2,32]{1,0:T(2,128)} %ids_ref.3) | copy-start | bytes 772
  2.0 17.3 %copy-start.8 = (s32[16]{0:T(128)S(1)}, s32[16]{0:T(128)}, u32[]{:S(2)}) copy-start(s32[16]{0:T(128)} %len_ref.1) | copy-start | bytes 196
  2.0 28.0 %all-to-all-start = ((f32[64,1,128]{2,1,0:T(1,128)}), f32[64,1,128]{2,1,0:T(1,128)S(1)}, u32[]{:S(2)}, u32[]{:S(2)}) async-start(f32[64,1,128]{2,1,0:T(1,128)} %bitcast.1), calls=%async_computation | async-start | bytes 65536 | tf_op jit(solution)/shard_map/all_to_all | solution.py:278
  19.3 0.8 copy-start.7
  30.1 30.3 %copy-start.2 = (bf16[128,512]{1,0:T(8,128)(2,1)S(1)}, bf16[128,512]{1,0:T(8,128)(2,1)}, u32[]{:S(2)}) copy-start(bf16[128,512]{1,0:T(8,128)(2,1)} %sk_ref.1) | copy-start | bytes 393220
  30.1 30.3 %copy-start.3 = (bf16[128,512]{1,0:T(8,128)(2,1)S(1)}, bf16[128,512]{1,0:T(8,128)(2,1)}, u32[]{:S(2)}) copy-start(bf16[128,512]{1,0:T(8,128)(2,1)} %sv_ref.1) | copy-start | bytes 393220
  30.7 29.7 %copy-start = (bf16[128,4096]{1,0:T(8,128)(2,1)S(1)}, bf16[128,4096]{1,0:T(8,128)(2,1)}, u32[]{:S(2)}) copy-start(bf16[128,4096]{1,0:T(8,128)(2,1)} %q_ref.1) | copy-start | bytes 3145732
  30.7 29.7 %copy-start.1 = (bf16[128,4096]{1,0:T(8,128)(2,1)S(1)}, bf16[128,4096]{1,0:T(8,128)(2,1)}, u32[]{:S(2)}) copy-start(bf16[128,4096]{1,0:T(8,128)(2,1)} %g_ref.1) | copy-start | bytes 3145732

commit v5 on v4

--- a/solution.py
+++ b/solution.py
@@ -73,6 +73,7 @@
     mask_ref,
     kv_ref,
     place_ref,
+    take_ref,
 ):
     rows = owners * CAP * plen
     width = CAP * n_local * plen
@@ -106,7 +107,9 @@
         asked = jnp.concatenate(
             [one(hits[n] & (locs[n] == picked)) for picked in (low, high)], axis=0
         )
-        place_ref[:, n * lanes : (n + 1) * lanes] = jnp.where(same, dot(who, asked), 0.0).astype(BF)
+        place = jnp.where(same, dot(who, asked), 0.0)
+        place_ref[:, n * lanes : (n + 1) * lanes] = place.astype(BF)
+        take_ref[n * lanes : (n + 1) * lanes] = place.T.astype(BF)
 
 
 def owner_kernel(owners, plen, req_ref, mask_ref, kv_ref, send_ref, table_ref):
@@ -127,6 +130,7 @@
 
 def attend_kernel(
     place_ref,
+    take_ref,
     recv_ref,
     q_ref,
     g_ref,
@@ -146,7 +150,7 @@
     n_query = sk_ref.shape[0] // q_len
     lanes = place_ref.shape[1] // n_query
     wide = group * q_len
-    kv_ref[...] = dot(place_ref[...], recv_ref[...], 0, 0).astype(BF)
+    kv_ref[...] = dot(take_ref[...], recv_ref[...]).astype(BF)
     causal = iota((q_len, wide), 0) <= iota((q_len, wide), 1) % q_len
     pairs = [(n, g) for n in range(n_query) for g in range(kv_heads)]
 
@@ -279,12 +283,13 @@
         request.reshape(owners, 1, width), "pas", split_axis=0, concat_axis=0, tiled=True
     ).reshape(owners, width)
 
-    mask, tables, place = call(
+    mask, tables, place, take = call(
         functools.partial(prepare_kernel, *dims),
         [
             sds((rows, width), BF),
             sds((width, 2 * kv_width), BF),
             sds((rows, n_query * lanes), BF),
+            sds((n_query * lanes, rows), BF),
         ],
         [SMEM] + [VMEM] * 3,
         "prepare",
@@ -306,11 +311,11 @@
             sds(suffix_values.shape, BF),
             sds((rows, 2 * kv_width), BF),
         ],
-        [VMEM] * 6,
+        [VMEM] * 7,
         "attend",
         limit=24,
         scratch=[pltpu.VMEM((n_query * lanes, 2 * kv_width), BF)] * 2,
-    )(place, recv, queries, grad_out, suffix_keys, suffix_values)
+    )(place, take, recv, queries, grad_out, suffix_keys, suffix_values)
     back = exchange(terms)
 
     sums = call(owner_sum_kernel, sds((n_local * plen, 2 * kv_width), BF), [VMEM] * 2, "owner_sum")(

time: 114 us -> 114 us (level)
  no operation moved by 1% of the time
where the time goes in v5:
time: 114 us
  blocking collectives  77.9 us (68%)
  starting transfers between devices  17.3 us (15%)
  waiting for transfers between devices  8.76 us (8%)
  Pallas kernels  7.84 us (7%)
  local copies, waits for them, and re-layouts  1.54 us (1%)
    all_to_all x2, blocking collectives, exchange(): lax.all_to_all(parts, 'pas', split_axis=0, concat_axis=0, tiled=True)  63.6 us
    all_to_all x1, starting transfers between devices, on_device(): lax.all_to_all(request.reshape(owners, 1, width), 'pas', split_axis=0, co...  17.3 us
    all_to_all x1, blocking collectives, on_device(): lax.all_to_all(sums.reshape(groups, n_local // groups * plen, 2 * kv_widt...  14.4 us
    all_to_all x1, waiting for transfers between devices, on_device(): lax.all_to_all(request.reshape(owners, 1, width), 'pas', split_axis=0, co...  8.76 us
    pallas_call x1, Pallas kernels, on_device(): call(attend_kernel, [sds(queries.shape, BF), sds(suffix_keys.shape, BF),...  4.44 us
  transfers between devices with their start and end apart: 1, of which 1 were waited for; matrix products, arithmetic and copies ran while one was open for 0% of the time, Pallas kernels for 1%

profile of v5, /device:TPU:1, one launch (start us, length us, event | category | flops | bytes accessed | tf_op | source)
XLA Modules:
  0.0 114.1 jit_solution(16213891745605338609)
XLA Ops:
  0.6 0.0 copy-start.4
  0.6 0.7 copy-done.4
  1.3 0.0 copy-start.6
  1.3 0.7 request.1
  2.0 0.0 copy-start.5
  2.0 0.0 copy-start.8
  2.0 17.3 %all-to-all-start = ((f32[64,1,128]{2,1,0:T(1,128)}), f32[64,1,128]{2,1,0:T(1,128)S(1)}, u32[]{:S(2)}, u32[]{:S(2)}) async-start(f32[64,1,128]{2,1,0:T(1,128)} %bitcast.1), calls=%async_computation | async-start | bytes 65536 | tf_op jit(solution)/shard_map/all_to_all | solution.py:282
  19.3 0.0 copy-done.6
  19.3 0.0 copy-done.5
  19.3 0.0 copy-done.8
  19.3 0.0 copy-start.7
  19.4 0.8 copy-done.7
  20.2 1.1 prepare.1
  21.3 8.8 %all-to-all-done = f32[64,1,128]{2,1,0:T(1,128)S(1)} async-done(((f32[64,1,128]{2,1,0:T(1,128)}), f32[64,1,128]{2,1,0:T(1,128)S(1)}, u32[]{:S(2)}, u32[]{:S(2)}) %all-to-all-start) | async-done | bytes 32800 | tf_op jit(solution)/shard_map/all_to_all | solution.py:282
  30.1 0.0 copy-start.2
  30.1 0.0 copy-start.3
  30.1 0.6 owner_gather.1
  30.7 0.0 copy-start
  30.7 0.0 copy-start.1
  30.7 29.7 %all_to_all.20 = bf16[64,8,1024]{2,1,0:T(8,128)(2,1)S(1)} all-to-all(bf16[64,8,1024]{2,1,0:T(8,128)(2,1)S(1)} %bitcast.12), channel_id=1, replica_groups=mesh['pas'=64,'qry'=8] {'pas'}, dimensions={0} | all-to-all | bytes 2097152 | tf_op jit(solution)/shard_map/all_to_all | solution.py:277
  60.4 0.0 copy-done.2
  60.4 0.0 copy-done.3
  60.4 0.0 copy-done
  60.4 0.0 copy-done.1
  60.4 4.4 %attend.1 = (bf16[128,4096]{1,0:T(8,128)(2,1)}, bf16[128,512]{1,0:T(8,128)(2,1)}, bf16[128,512]{1,0:T(8,128)(2,1)}, bf16[512,1024]{1,0:T(8,128)(2,1)S(1)}) custom-call(bf16[512,256]{1,0:T(8,128)(2,1)S(1)} %get-tuple-element.17.place_ref, bf16[256,512]{1,0:T(8,128)(2,1)S(1)} %get-tuple-element.18.take_ref, bf16[512,1024]{1,0:T(8,128)(2,1)S(1)} %bitcast.10, ...), custom_call_target="tpu_custom_call" | custom-call | tf_op jit(solution)/shard_map/attend/pallas_call | solution.py:306
  64.8 33.9 %all_to_all.21 = bf16[64,8,1024]{2,1,0:T(8,128)(2,1)S(1)} all-to-all(bf16[64,8,1024]{2,1,0:T(8,128)(2,1)S(1)} %bitcast.11), channel_id=1, replica_groups=mesh['pas'=64,'qry'=8] {'pas'}, dimensions={0} | all-to-all | bytes 2097152 | tf_op jit(solution)/shard_map/all_to_all | solution.py:277
  98.8 0.3 owner_sum.1
  99.1 14.4 %all_to_all.22.parts_ref = bf16[8,8,1024]{2,1,0:T(8,128)(2,1)S(1)} all-to-all(bf16[8,8,1024]{2,1,0:T(8,128)(2,1)S(1)} %bitcast.13), channel_id=1, replica_groups=mesh['pas'=64,'qry'=8] {'qry'}, dimensions={0} | all-to-all | bytes 262144 | tf_op jit(solution)/shard_map/all_to_all | solution.py:324
  113.5 0.6 final_sum.1
Async XLA Ops:
  0.6 0.7 copy-start.4
  1.3 18.0 %copy-start.6 = (bf16[16,4,512]{2,1,0:T(4,128)(2,1)S(1)}, bf16[16,4,512]{2,1,0:T(4,128)(2,1)}, u32[]{:S(2)}) copy-start(bf16[16,4,512]{2,1,0:T(4,128)(2,1)} %pk_ref.1) | copy-start | bytes 196612
  2.0 17.3 %copy-start.5 = (s32[2,32]{1,0:T(2,128)S(1)}, s32[2,32]{1,0:T(2,128)}, u32[]{:S(2)}) copy-start(s32[2,32]{1,0:T(2,128)} %ids_ref.3) | copy-start | bytes 772
  2.0 17.3 %copy-start.8 = (s32[16]{0:T(128)S(1)}, s32[16]{0:T(128)}, u32[]{:S(2)}) copy-start(s32[16]{0:T(128)} %len_ref.1) | copy-start | bytes 196
  2.0 28.0 %all-to-all-start = ((f32[64,1,128]{2,1,0:T(1,128)}), f32[64,1,128]{2,1,0:T(1,128)S(1)}, u32[]{:S(2)}, u32[]{:S(2)}) async-start(f32[64,1,128]{2,1,0:T(1,128)} %bitcast.1), calls=%async_computation | async-start | bytes 65536 | tf_op jit(solution)/shard_map/all_to_all | solution.py:282
  19.3 0.8 copy-start.7
  30.1 30.3 %copy-start.2 = (bf16[128,512]{1,0:T(8,128)(2,1)S(1)}, bf16[128,512]{1,0:T(8,128)(2,1)}, u32[]{:S(2)}) copy-start(bf16[128,512]{1,0:T(8,128)(2,1)} %sk_ref.1) | copy-start | bytes 393220
  30.1 30.3 %copy-start.3 = (bf16[128,512]{1,0:T(8,128)(2,1)S(1)}, bf16[128,512]{1,0:T(8,128)(2,1)}, u32[]{:S(2)}) copy-start(bf16[128,512]{1,0:T(8,128)(2,1)} %sv_ref.1) | copy-start | bytes 393220
  30.7 29.7 %copy-start = (bf16[128,4096]{1,0:T(8,128)(2,1)S(1)}, bf16[128,4096]{1,0:T(8,128)(2,1)}, u32[]{:S(2)}) copy-start(bf16[128,4096]{1,0:T(8,128)(2,1)} %q_ref.1) | copy-start | bytes 3145732
  30.7 29.7 %copy-start.1 = (bf16[128,4096]{1,0:T(8,128)(2,1)S(1)}, bf16[128,4096]{1,0:T(8,128)(2,1)}, u32[]{:S(2)}) copy-start(bf16[128,4096]{1,0:T(8,128)(2,1)} %g_ref.1) | copy-start | bytes 3145732
